TPU v7x, 32 devices: a whole 2x2x4 slice. The times are simulated.
32 devices in a mesh: groups: 2 (over y), ep: 8 (over z, x), edp: 2 (over core).
Axes of the slice: x: 2, y: 2, z: 4, core: 2. Of those that a mesh axis runs over, the one named last changes fastest.
Arguments:
- hidden_in: bfloat16 [4096, 2048], P(('groups', 'ep', 'edp')), parts along dimension 0, may hold values from -6 to 6
- out_grad: bfloat16 [4096, 2048], P(('groups', 'ep', 'edp')), parts along dimension 0, may hold values from -0.59765625 to 0.59765625
- routes: int32 [4096, 2], P(('groups', 'ep', 'edp')), parts along dimension 0, may hold values from 0 to 7, all different within a row; in each aligned block of 128 rows (0 to 127, 128 to 255, ...) at most 64 rows name the same one
- probs: float32 [4096, 2], P(('groups', 'ep', 'edp')), parts along dimension 0, may hold values from 0.05 to 1
- w_gate: bfloat16 [8, 2048, 768], P('ep', 'edp'), may hold values from -0.125 to 0.125
- w_up: bfloat16 [8, 2048, 768], P('ep', 'edp'), may hold values from -0.125 to 0.125
- w_down: bfloat16 [8, 768, 2048], P('ep', 'edp'), may hold values from -0.21875 to 0.21875
Outputs:
- input_grad: bfloat16 [4096, 2048], P(('groups', 'ep', 'edp')), parts along dimension 0
- prob_grad: float32 [4096, 2], P(('groups', 'ep', 'edp')), parts along dimension 0
- gate_wgrad: bfloat16 [16, 2048, 768], P(('groups', 'ep'), 'edp'), parts along dimension 0
- up_wgrad: bfloat16 [16, 2048, 768], P(('groups', 'ep'), 'edp'), parts along dimension 0
- down_wgrad: bfloat16 [16, 768, 2048], P(('groups', 'ep'), 'edp'), parts along dimension 0
There are 2 independent parts, one for each index of `groups`. A program takes and returns all parts, laid end to end along the dimension named above; an argument that names none is the same for every part. Nothing has to cross between parts.
Inputs may be any that keep to these rules, and one draw needn't show every extreme that they name: `routes`: each row names 2 different experts; among the rows of one device no expert is named more than 64 times.
All inputs are finite; a program needn't handle non-finite values.
Results may differ from a plain program's by a relative error of at most 0.015.
Values may be sent and summed in bfloat16 or wider, within the bound.
A program may use at most 128 MiB of HBM per device.

v0:
```python
import jax
import jax.numpy as jnp
from jax import lax
from jax.sharding import PartitionSpec as P


def forward_part(rows_in, gate_full, up_full, down_full):
    gate = jnp.dot(rows_in, gate_full, preferred_element_type=jnp.float32)
    upper = jnp.dot(rows_in, up_full, preferred_element_type=jnp.float32)
    sigma = jax.nn.sigmoid(gate)
    active = gate * sigma
    hidden = (active * upper).astype(jnp.bfloat16)
    expert_out = jnp.dot(hidden, down_full, preferred_element_type=jnp.float32)
    return (gate, upper, sigma, active, hidden, expert_out)


def backward_part(state, rows_grad, weights_row, gate_full, up_full, down_full):
    gate, upper, sigma, active, hidden, expert_out = state
    grad_wide = rows_grad.astype(jnp.float32)
    prob_grad = jnp.sum(expert_out * grad_wide, axis=1)
    scaled = (weights_row[:, None] * grad_wide).astype(jnp.bfloat16)
    hidden_grad = lax.dot_general(
        scaled, down_full, (((1,), (1,)), ((), ())), preferred_element_type=jnp.float32
    )
    up_grad = (hidden_grad * active).astype(jnp.bfloat16)
    gate_grad = (hidden_grad * upper * sigma * (1.0 + gate * (1.0 - sigma))).astype(jnp.bfloat16)
    row_grad = lax.dot_general(
        gate_grad, gate_full, (((1,), (1,)), ((), ())), preferred_element_type=jnp.float32
    )
    row_grad = row_grad + lax.dot_general(
        up_grad, up_full, (((1,), (1,)), ((), ())), preferred_element_type=jnp.float32
    )
    return (scaled, gate_grad, up_grad, row_grad.astype(jnp.bfloat16), prob_grad)


def local(hidden_in, out_grad, routes, probs, w_gate, w_up, w_down):
    tok_rows, top_k = routes.shape
    width = hidden_in.shape[1]
    ep_size = lax.axis_size("ep")
    expert_count = ep_size * w_gate.shape[0]
    slot_cap = max(8, 2 * tok_rows * top_k // expert_count)
    flat_routes = routes.reshape(-1)
    onehot = (flat_routes[:, None] == jnp.arange(expert_count, dtype=jnp.int32)[None, :]).astype(
        jnp.int32
    )
    running = jnp.cumsum(onehot, axis=0) - 1
    position = jnp.sum(running * onehot, axis=1)
    destination = flat_routes * slot_cap + position
    token_ids = jnp.arange(tok_rows * top_k, dtype=jnp.int32) // top_k
    slot_room = expert_count * slot_cap
    send_in = (
        jnp.zeros((slot_room, width), hidden_in.dtype).at[destination].set(hidden_in[token_ids])
    )
    send_grad = (
        jnp.zeros((slot_room, width), out_grad.dtype).at[destination].set(out_grad[token_ids])
    )
    send_weights = jnp.zeros((slot_room,), probs.dtype).at[destination].set(probs.reshape(-1))
    send_in = send_in.reshape(expert_count, slot_cap, width)
    send_grad = send_grad.reshape(expert_count, slot_cap, width)
    send_weights = send_weights.reshape(expert_count, slot_cap)
    gate_full, up_full, down_full = (
        lax.all_gather(w_gate[0], "edp", axis=0, tiled=True),
        lax.all_gather(w_up[0], "edp", axis=0, tiled=True),
        lax.all_gather(w_down[0], "edp", axis=0, tiled=True),
    )
    recv_in, recv_grad, recv_weights = (
        lax.all_to_all(send_in, "ep", split_axis=0, concat_axis=0, tiled=True),
        lax.all_to_all(send_grad, "ep", split_axis=0, concat_axis=0, tiled=True),
        lax.all_to_all(
            send_weights.astype(jnp.bfloat16), "ep", split_axis=0, concat_axis=0, tiled=True
        ).astype(send_weights.dtype),
    )
    rows_in = recv_in.reshape(-1, width)
    state = forward_part(rows_in, gate_full, up_full, down_full)
    rows_grad = recv_grad.reshape(-1, width)
    weights_row = recv_weights.reshape(-1)
    hidden = state[4]
    scaled, gate_grad, up_grad, row_grad, prob_grad = backward_part(
        state, rows_grad, weights_row, gate_full, up_full, down_full
    )
    back_rows, back_probs = (
        lax.all_to_all(
            row_grad.reshape(ep_size, slot_cap, width),
            "ep",
            split_axis=0,
            concat_axis=0,
            tiled=True,
        ),
        lax.all_to_all(
            prob_grad.reshape(ep_size, slot_cap).astype(jnp.bfloat16),
            "ep",
            split_axis=0,
            concat_axis=0,
            tiled=True,
        ).astype(jnp.float32),
    )
    picked_rows = back_rows.reshape(-1, width)[destination]
    input_grad = jnp.sum(
        picked_rows.astype(jnp.float32).reshape(tok_rows, top_k, width), axis=1
    ).astype(jnp.bfloat16)
    prob_out = back_probs.reshape(-1)[destination].reshape(tok_rows, top_k)
    contract = (((0,), (0,)), ((), ()))
    gate_term = lax.dot_general(rows_in, gate_grad, contract, preferred_element_type=jnp.float32)
    up_term = lax.dot_general(rows_in, up_grad, contract, preferred_element_type=jnp.float32)
    down_term = lax.dot_general(hidden, scaled, contract, preferred_element_type=jnp.float32)
    gate_share, up_share, down_share = (
        lax.psum_scatter(
            gate_term.astype(jnp.bfloat16), "edp", scatter_dimension=0, tiled=True
        ).astype(jnp.float32),
        lax.psum_scatter(
            up_term.astype(jnp.bfloat16), "edp", scatter_dimension=0, tiled=True
        ).astype(jnp.float32),
        lax.psum_scatter(
            down_term.astype(jnp.bfloat16), "edp", scatter_dimension=0, tiled=True
        ).astype(jnp.float32),
    )
    gate_wgrad = gate_share.astype(jnp.bfloat16)[None]
    up_wgrad = up_share.astype(jnp.bfloat16)[None]
    down_wgrad = down_share.astype(jnp.bfloat16)[None]
    return (input_grad, prob_out, gate_wgrad, up_wgrad, down_wgrad)


def solution(mesh):
    placed = (
        P(("groups", "ep", "edp"), None),
        P(("groups", "ep", "edp"), None),
        P(("groups", "ep", "edp"), None),
        P(("groups", "ep", "edp"), None),
        P("ep", "edp", None),
        P("ep", "edp", None),
        P("ep", "edp", None),
    )
    return jax.shard_map(
        local,
        mesh=mesh,
        in_specs=placed,
        out_specs=(
            P(("groups", "ep", "edp"), None),
            P(("groups", "ep", "edp"), None),
            P(("groups", "ep"), "edp", None),
            P(("groups", "ep"), "edp", None),
            P(("groups", "ep"), "edp", None),
        ),
        check_vma=False,
    )
```

profile of v0, /device:TPU:0, one launch (start us, length us, event | category | flops | bytes accessed | tf_op | source)
XLA Modules:
  0.0 249.9 jit_solution(5835517970506048567)
XLA Ops:
  7.2 0.7 all-gather.11.cloned.1.call-update
  7.9 0.8 copy.18
  9.0 0.7 broadcast_multiply_fusion
  10.8 0.8 copy.20
  11.8 1.4 scatter_custom_fusion
  13.9 7.3 %all-to-all-start = ((bf16[8,1,64]{2,1,0:T(2,128)(2,1)}), bf16[8,1,64]{2,1,0:T(2,128)(2,1)S(1)}, u32[]{:S(2)}, u32[]{:S(2)}) async-start(bf16[8,1,64]{2,1,0:T(2,128)(2,1)} %convert_element_type.109), calls=%async_computation | async-start | bytes 8192 | tf_op jit(solution)/shard_map/all_to_all | solution.py:69
  21.2 7.0 %scatter_custom_fusion.2 = bf16[512,2048]{1,0:T(8,128)(2,1)} fusion(s32[256]{0:T(256)S(1)} %bitcast.63, bf16[128,2048]{1,0:T(8,128)(2,1)S(1)} %copy-done, s32[1024]{0:T(1024)S(1)} %pad_clamp_fusion.1, bf16[]{:T(256)} %constant.34.clone.1), kind=kCustom, calls=%fused_computation.31 | custom fusion | bytes 2097154 | tf_op jit(solution)/shard_map/scatter | solution.py:52
  28.2 6.0 %all-to-all-start.2 = ((bf16[8,64,2048]{2,1,0:T(8,128)(2,1)}), bf16[8,64,2048]{2,1,0:T(8,128)(2,1)S(1)}, u32[]{:S(2)}, u32[]{:S(2)}) async-start(bf16[8,64,2048]{2,1,0:T(8,128)(2,1)} %bitcast.8), calls=%async_computation.2 | async-start | bytes 4194304 | tf_op jit(solution)/shard_map/all_to_all | solution.py:67
  35.0 7.2 %scatter_custom_fusion.1 = bf16[512,2048]{1,0:T(8,128)(2,1)} fusion(s32[256]{0:T(256)S(1)} %bitcast.64, bf16[128,2048]{1,0:T(8,128)(2,1)} %param.8, s32[1024]{0:T(1024)S(1)} %pad_clamp_fusion.1, bf16[]{:T(256)} %constant.34.clone.1), kind=kCustom, calls=%fused_computation.33 | custom fusion | bytes 2097664 | tf_op jit(solution)/shard_map/scatter | solution.py:55
  42.2 39.7 %all-to-all-done.2 = bf16[8,64,2048]{2,1,0:T(8,128)(2,1)S(1)} async-done(((bf16[8,64,2048]{2,1,0:T(8,128)(2,1)}), bf16[8,64,2048]{2,1,0:T(8,128)(2,1)S(1)}, u32[]{:S(2)}, u32[]{:S(2)}) %all-to-all-start.2) | async-done | bytes 2097184 | tf_op jit(solution)/shard_map/all_to_all | solution.py:67
  81.9 1.3 copy-done.1
  83.2 3.6 %all-to-all-start.1 = ((bf16[8,64,2048]{2,1,0:T(8,128)(2,1)}), bf16[8,64,2048]{2,1,0:T(8,128)(2,1)S(1)}, u32[]{:S(2)}, u32[]{:S(2)}) async-start(bf16[8,64,2048]{2,1,0:T(8,128)(2,1)} %bitcast.56), calls=%async_computation.1 | async-start | bytes 4194304 | tf_op jit(solution)/shard_map/all_to_all | solution.py:68
  88.0 5.4 %fusion.4 = f32[512,768]{1,0:T(8,128)} fusion(bf16[512,2048]{1,0:T(8,128)(2,1)} %bitcast.57, bf16[1,2048,768]{2,1,0:T(8,128)(2,1)} %all-gather.11.cloned.1.call-done), kind=kOutput, calls=%fused_computation.17 | convolution fusion | flops 1610612736 | bytes 6815744 | tf_op jit(solution)/shard_map/dot_general | solution.py:8
  93.4 41.9 %all-to-all-done.1 = bf16[8,64,2048]{2,1,0:T(8,128)(2,1)S(1)} async-done(((bf16[8,64,2048]{2,1,0:T(8,128)(2,1)}), bf16[8,64,2048]{2,1,0:T(8,128)(2,1)S(1)}, u32[]{:S(2)}, u32[]{:S(2)}) %all-to-all-start.1) | async-done | bytes 2097184 | tf_op jit(solution)/shard_map/all_to_all | solution.py:68
  135.3 1.7 fusion
  137.0 5.5 %fusion.11 = f32[512,768]{1,0:T(8,128)} fusion(bf16[512,2048]{1,0:T(8,128)(2,1)} %fusion, bf16[1,768,2048]{2,1,0:T(8,128)(2,1)} %all-gather.7.cloned.1.call-done), kind=kOutput, calls=%fused_computation.24 | convolution fusion | flops 1610612736 | bytes 6815744 | tf_op jit(solution)/shard_map/dot_general | solution.py:22
  142.5 6.6 %multiply_convert_fusion = (bf16[512,768]{1,0:T(8,128)(2,1)S(1)}, bf16[512,768]{1,0:T(8,128)(2,1)}, bf16[512,768]{1,0:T(8,128)(2,1)S(1)}) fusion(f32[512,768]{1,0:T(8,128)} %fusion.4, f32[512,768]{1,0:T(8,128)} %fusion.11, bf16[512,2048]{1,0:T(8,128)(2,1)} %bitcast.58, bf16[1,2048,768]{2,1,0:T(8,128)(2,1)} %all-gather.9.cloned.1.call-done), kind=kOutput, calls=%fused_computation.26 | convolution fusion | flops 1616510976 | bytes 10747904 | tf_op jit(solution)/shard_map/dot_general | solution.py:9
  149.2 0.9 copy-done.4
  150.1 3.5 %convolution_convert_fusion = bf16[768,2048]{1,0:T(8,128)(2,1)} fusion(bf16[512,768]{1,0:T(8,128)(2,1)S(1)} %get-tuple-element.15, bf16[512,2048]{1,0:T(8,128)(2,1)S(1)} %copy-done.2), kind=kOutput, calls=%fused_computation.12 | convolution fusion | flops 1612185600 | bytes 6029312 | tf_op jit(solution)/shard_map/dot_general | solution.py:105
  153.7 5.1 %convolution_convert_fusion.1 = bf16[2048,768]{1,0:T(8,128)(2,1)} fusion(bf16[512,2048]{1,0:T(8,128)(2,1)} %bitcast.59, bf16[512,768]{1,0:T(8,128)(2,1)S(1)} %get-tuple-element.17), kind=kOutput, calls=%fused_computation.13 | convolution fusion | flops 1612185600 | bytes 6029312 | tf_op jit(solution)/shard_map/dot_general | solution.py:104
  159.1 5.3 %convolution_convert_fusion.2 = bf16[2048,768]{1,0:T(8,128)(2,1)} fusion(bf16[512,2048]{1,0:T(8,128)(2,1)} %bitcast.60, bf16[512,768]{1,0:T(8,128)(2,1)} %get-tuple-element.16), kind=kOutput, calls=%fused_computation.14 | convolution fusion | flops 1612185600 | bytes 6029312 | tf_op jit(solution)/shard_map/dot_general | solution.py:103
  164.4 4.0 %fusion.1 = bf16[512]{0:T(512)(128)(2,1)S(1)} fusion(bf16[512,2048]{1,0:T(8,128)(2,1)S(1)} %bitcast.55, bf16[512,768]{1,0:T(8,128)(2,1)} %copy-done.4, bf16[1,768,2048]{2,1,0:T(8,128)(2,1)} %all-gather.7.cloned.1.call-done), kind=kOutput, calls=%fused_computation.10 | convolution fusion | flops 1613757952 | bytes 6030336 | tf_op jit(solution)/shard_map/dot_general | solution.py:13
  168.5 0.7 convert_element_type.110
  169.2 4.2 %all-to-all-start.4 = ((bf16[8,1,64]{2,1,0:T(2,128)(2,1)}), bf16[8,1,64]{2,1,0:T(2,128)(2,1)S(1)}, u32[]{:S(2)}, u32[]{:S(2)}) async-start(bf16[8,1,64]{2,1,0:T(2,128)(2,1)} %convert_element_type.110), calls=%async_computation.4 | async-start | bytes 8192 | tf_op jit(solution)/shard_map/all_to_all | solution.py:89
  173.4 4.4 %fusion.2 = f32[512,2048]{1,0:T(8,128)S(1)} fusion(bf16[512,768]{1,0:T(8,128)(2,1)} %get-tuple-element.16, bf16[1,2048,768]{2,1,0:T(8,128)(2,1)} %all-gather.11.cloned.1.call-done), kind=kOutput, calls=%fused_computation.15 | convolution fusion | flops 1610612736 | bytes 8126464 | tf_op jit(solution)/shard_map/dot_general | solution.py:27
  177.8 3.2 %add_convert_fusion = bf16[512,2048]{1,0:T(8,128)(2,1)} fusion(f32[512,2048]{1,0:T(8,128)S(1)} %fusion.2, bf16[512,768]{1,0:T(8,128)(2,1)S(1)} %get-tuple-element.17, bf16[1,2048,768]{2,1,0:T(8,128)(2,1)S(1)} %copy-done.3), kind=kOutput, calls=%fused_computation.11 | convolution fusion | flops 1612709888 | bytes 10223616 | tf_op jit(solution)/shard_map/dot_general | solution.py:30
  181.0 5.9 %all-to-all-start.3 = ((bf16[8,64,2048]{2,1,0:T(8,128)(2,1)}), bf16[8,64,2048]{2,1,0:T(8,128)(2,1)S(1)}, u32[]{:S(2)}, u32[]{:S(2)}) async-start(bf16[8,64,2048]{2,1,0:T(8,128)(2,1)} %bitcast.61), calls=%async_computation.3 | async-start | bytes 4194304 | tf_op jit(solution)/shard_map/all_to_all | solution.py:82
  187.0 1.9 gather_fusion.1
  189.7 45.7 %all-to-all-done.3 = bf16[8,64,2048]{2,1,0:T(8,128)(2,1)S(1)} async-done(((bf16[8,64,2048]{2,1,0:T(8,128)(2,1)}), bf16[8,64,2048]{2,1,0:T(8,128)(2,1)S(1)}, u32[]{:S(2)}, u32[]{:S(2)}) %all-to-all-start.3) | async-done | bytes 2097184 | tf_op jit(solution)/shard_map/all_to_all | solution.py:82
  235.4 2.3 gather_fusion
  237.7 1.7 gather.17
  239.5 3.6 %reduce_sum.34 = bf16[128,2048]{1,0:T(8,128)(2,1)} reduce(bf16[128,2,2048]{2,1,0:T(2,128)(2,1)S(1)} %gather.17, bf16[]{:T(256)} %constant.34.clone.1), dimensions={1}, to_apply=%region_6.7 | reduce | flops 262144 | bytes 1572866 | tf_op jit(solution)/shard_map/reduce_sum | solution.py:98
  (50 shorter events, 5.4 us)
Async XLA Ops:
  7.2 14.0 %copy-start = (bf16[128,2048]{1,0:T(8,128)(2,1)S(1)}, bf16[128,2048]{1,0:T(8,128)(2,1)}, u32[]{:S(2)}) copy-start(bf16[128,2048]{1,0:T(8,128)(2,1)} %param.7) | copy-start | bytes 1572868
  7.2 80.8 %all-gather.11.cloned.1.call-start = ((), (), s32[]{:S(2)}) async-start(), calls=%async_computation.13 | async-start | bytes 4718592 | tf_op jit(solution)/shard_map/all_gather | solution.py:62
  13.9 14.3 %all-to-all-start = ((bf16[8,1,64]{2,1,0:T(2,128)(2,1)}), bf16[8,1,64]{2,1,0:T(2,128)(2,1)S(1)}, u32[]{:S(2)}, u32[]{:S(2)}) async-start(bf16[8,1,64]{2,1,0:T(2,128)(2,1)} %convert_element_type.109), calls=%async_computation | async-start | bytes 8192 | tf_op jit(solution)/shard_map/all_to_all | solution.py:69
  28.2 53.7 %all-to-all-start.2 = ((bf16[8,64,2048]{2,1,0:T(8,128)(2,1)}), bf16[8,64,2048]{2,1,0:T(8,128)(2,1)S(1)}, u32[]{:S(2)}, u32[]{:S(2)}) async-start(bf16[8,64,2048]{2,1,0:T(8,128)(2,1)} %bitcast.8), calls=%async_computation.2 | async-start | bytes 4194304 | tf_op jit(solution)/shard_map/all_to_all | solution.py:67
  34.2 102.8 %all-gather.7.cloned.1.call-start = ((), (), s32[]{:S(2)}) async-start(), calls=%async_computation.11 | async-start | bytes 4718592 | tf_op jit(solution)/shard_map/all_gather | solution.py:64
  81.9 1.3 copy-start.1
  83.2 52.1 %all-to-all-start.1 = ((bf16[8,64,2048]{2,1,0:T(8,128)(2,1)}), bf16[8,64,2048]{2,1,0:T(8,128)(2,1)S(1)}, u32[]{:S(2)}, u32[]{:S(2)}) async-start(bf16[8,64,2048]{2,1,0:T(8,128)(2,1)} %bitcast.56), calls=%async_computation.1 | async-start | bytes 4194304 | tf_op jit(solution)/shard_map/all_to_all | solution.py:68
  86.9 55.7 %all-gather.9.cloned.1.call-start = ((), (), s32[]{:S(2)}) async-start(), calls=%async_computation.12 | async-start | bytes 4718592 | tf_op jit(solution)/shard_map/all_gather | solution.py:63
  87.6 155.5 %reduce-scatter.8.cloned.1.call-start = ((), (), s32[]{:S(2)}) async-start(), calls=%async_computation.10 | async-start | bytes 4718592 | tf_op jit(solution)/shard_map/reduce_scatter | solution.py:113
  142.5 7.6 %copy-start.2 = (bf16[512,2048]{1,0:T(8,128)(2,1)S(1)}, bf16[512,2048]{1,0:T(8,128)(2,1)}, u32[]{:S(2)}) copy-start(bf16[512,2048]{1,0:T(8,128)(2,1)} %fusion) | copy-start | bytes 6291460
  149.2 0.9 copy-start.4
  153.6 89.5 %reduce-scatter.6.cloned.1.call-start = ((), (), s32[]{:S(2)}) async-start(), calls=%async_computation.9 | async-start | bytes 4718592 | tf_op jit(solution)/shard_map/reduce_scatter | solution.py:110
  158.8 84.3 %reduce-scatter.4.cloned.1.call-start = ((), (), s32[]{:S(2)}) async-start(), calls=%async_computation.8 | async-start | bytes 4718592 | tf_op jit(solution)/shard_map/reduce_scatter | solution.py:107
  169.2 11.8 %all-to-all-start.4 = ((bf16[8,1,64]{2,1,0:T(2,128)(2,1)}), bf16[8,1,64]{2,1,0:T(2,128)(2,1)S(1)}, u32[]{:S(2)}, u32[]{:S(2)}) async-start(bf16[8,1,64]{2,1,0:T(2,128)(2,1)} %convert_element_type.110), calls=%async_computation.4 | async-start | bytes 8192 | tf_op jit(solution)/shard_map/all_to_all | solution.py:89
  173.4 4.4 %copy-start.3 = (bf16[1,2048,768]{2,1,0:T(8,128)(2,1)S(1)}, bf16[1,2048,768]{2,1,0:T(8,128)(2,1)}, u32[]{:S(2)}) copy-start(bf16[1,2048,768]{2,1,0:T(8,128)(2,1)} %all-gather.9.cloned.1.call-done) | copy-start | bytes 9437188
  181.0 54.4 %all-to-all-start.3 = ((bf16[8,64,2048]{2,1,0:T(8,128)(2,1)}), bf16[8,64,2048]{2,1,0:T(8,128)(2,1)S(1)}, u32[]{:S(2)}, u32[]{:S(2)}) async-start(bf16[8,64,2048]{2,1,0:T(8,128)(2,1)} %bitcast.61), calls=%async_computation.3 | async-start | bytes 4194304 | tf_op jit(solution)/shard_map/all_to_all | solution.py:82
Sparse Core Ops, SparseCore 0:
  9.6 14.8 all-gather.10
  36.6 13.5 all-gather.6
  89.2 13.5 all-gather.8
  153.7 9.9 reduce-scatter.7
  166.5 12.0 reduce-scatter.5
  181.3 12.0 reduce-scatter.3
where the time goes:
time: 251 us; the launch traced here: 250 us
  waiting for transfers between devices  129 us (51%)
  matrix products  43.1 us (17%)
  local copies, waits for them, and re-layouts  28.7 us (11%)
  starting transfers between devices  27.9 us (11%)
  between operations  14.2 us (6%)
  other arithmetic  6.84 us (3%)
    all_to_all x1, waiting for transfers between devices, local(): lax.all_to_all(row_grad.reshape(ep_size, slot_cap, width), 'ep', split_ax...  45.7 us
    all_to_all x1, waiting for transfers between devices, local(): lax.all_to_all(send_grad, 'ep', split_axis=0, concat_axis=0, tiled=True)  41.9 us
    all_to_all x1, waiting for transfers between devices, local(): lax.all_to_all(send_in, 'ep', split_axis=0, concat_axis=0, tiled=True)  39.7 us
    all_to_all x1, starting transfers between devices, local(): lax.all_to_all(send_weights.astype(jnp.bfloat16), 'ep', split_axis=0, con...  7.25 us
    scatter x1, local copies, waits for them, and re-layouts, local(): jnp.zeros((slot_room, width), out_grad.dtype).at[destination]  7.21 us
    scatter x1, local copies, waits for them, and re-layouts, local(): jnp.zeros((slot_room, width), hidden_in.dtype).at[destination]  7.05 us
    dot_general x1, matrix products, forward_part(): upper = jnp.dot(rows_in, up_full, preferred_element_type=jnp.float32)  6.65 us
    all_to_all x1, starting transfers between devices, local(): lax.all_to_all(send_in, 'ep', split_axis=0, concat_axis=0, tiled=True)  6 us
  transfers between devices with their start and end apart: 11, of which 3 were waited for; matrix products, arithmetic and copies ran while one was open for 27% of the time, Pallas kernels for 0%

commit v1 on v0

v1 whole, which is shorter than its diff:
```python
import jax
import jax.numpy as jnp
from jax import lax
from jax.sharding import PartitionSpec as P

F32 = jnp.float32
BF16 = jnp.bfloat16
LANE = 128


def dot(a, b, dims):
    return lax.dot_general(a, b, (dims, ((), ())), preferred_element_type=F32)


def routing(routes, probs, experts, cap):
    tok, top = routes.shape
    picks = routes[:, :, None] == jnp.arange(experts, dtype=jnp.int32)[None, None, :]
    chosen = jnp.any(picks, axis=1)
    weight = jnp.sum(jnp.where(picks, probs[:, :, None], 0.0), axis=1)
    order = jnp.arange(tok, dtype=jnp.int32)
    earlier = (order[:, None] > order[None, :]).astype(BF16)
    place = dot(earlier, chosen.astype(BF16), ((1,), (0,))).astype(jnp.int32)
    place = jnp.where(chosen, place, -1)
    slot = jnp.arange(cap, dtype=jnp.int32)
    select = place.T[:, None, :] == slot[None, :, None]
    return picks, select, weight


def local(hidden_in, out_grad, routes, probs, w_gate, w_up, w_down):
    tok, top = routes.shape
    width = hidden_in.shape[1]
    ep = lax.axis_size("ep")
    experts = ep * w_gate.shape[0]
    cap = max(8, 2 * tok * top // experts)
    rows = experts * cap
    picks, select, weight = routing(routes, probs, experts, cap)
    select_rows = select.reshape(rows, tok).astype(BF16)
    row_weight = jnp.sum(jnp.where(select, weight.T[:, None, :], 0.0), axis=2).reshape(rows, 1)
    send_in = dot(select_rows, hidden_in, ((1,), (0,))).astype(BF16)
    send_grad = dot(select_rows, out_grad, ((1,), (0,))).astype(BF16)
    send_grad = jnp.concatenate(
        [send_grad, jnp.broadcast_to(row_weight.astype(BF16), (rows, LANE))], axis=1
    )

    def swap(value):
        return lax.all_to_all(
            value.reshape(experts, cap, -1), "ep", split_axis=0, concat_axis=0, tiled=True
        ).reshape(rows, -1)

    gate_full, up_full, down_full = (
        lax.all_gather(w[0], "edp", axis=0, tiled=True) for w in (w_gate, w_up, w_down)
    )
    rows_in = swap(send_in)
    got = swap(send_grad)
    rows_grad = got[:, :width]
    p = got[:, width : width + 1].astype(F32)
    gate = dot(rows_in, gate_full, ((1,), (0,)))
    upper = dot(rows_in, up_full, ((1,), (0,)))
    sigma = jax.nn.sigmoid(gate)
    active = gate * sigma
    hidden = active * upper
    plain = dot(rows_grad, down_full, ((1,), (1,)))
    prob_grad = jnp.sum(hidden * plain, axis=1, keepdims=True)
    hidden_grad = plain * p
    up_grad = (hidden_grad * active).astype(BF16)
    gate_grad = (hidden_grad * upper * sigma * (1.0 + gate * (1.0 - sigma))).astype(BF16)
    scaled_hidden = (hidden * p).astype(BF16)
    row_grad = dot(gate_grad, gate_full, ((1,), (1,))) + dot(up_grad, up_full, ((1,), (1,)))
    row_grad = jnp.concatenate(
        [row_grad.astype(BF16), jnp.broadcast_to(prob_grad.astype(BF16), (rows, LANE))], axis=1
    )
    row_grad, gate_grad, up_grad, scaled_hidden = lax.optimization_barrier(
        (row_grad, gate_grad, up_grad, scaled_hidden)
    )
    back = swap(row_grad)
    input_grad = dot(select_rows, back[:, :width], ((0,), (0,))).astype(BF16)
    back_prob = back[:, width].astype(F32).reshape(experts, cap, 1)
    by_expert = jnp.sum(jnp.where(select, back_prob, 0.0), axis=1).T
    prob_out = jnp.sum(jnp.where(picks, by_expert[:, None, :], 0.0), axis=2)

    def share(a, b):
        term = dot(a, b, ((0,), (0,))).astype(BF16)
        return lax.psum_scatter(term, "edp", scatter_dimension=0, tiled=True)[None]

    return (
        input_grad,
        prob_out,
        share(rows_in, gate_grad),
        share(rows_in, up_grad),
        share(scaled_hidden, rows_grad),
    )


def solution(mesh):
    tokens = P(("groups", "ep", "edp"), None)
    weights = P("ep", "edp", None)
    grads = P(("groups", "ep"), "edp", None)
    return jax.shard_map(
        local,
        mesh=mesh,
        in_specs=(tokens,) * 4 + (weights,) * 3,
        out_specs=(tokens, tokens, grads, grads, grads),
        check_vma=False,
    )
```

time: 251 us -> 224 us (0.89)
  blocking collectives: 0 us -> 55.6 us
  waiting for transfers between devices: 129 us -> 91.8 us
  local copies, waits for them, and re-layouts: 28.7 us -> 5.35 us
  starting transfers between devices: 27.9 us -> 11.7 us
  other arithmetic: 6.84 us -> 3.67 us
    all_to_all x0 -> x1, blocking collectives: none -> 55.6 us  [swap(): lax.all_to_all(value.reshape(experts, cap, -1), 'ep', split_axis=0, conca...]
    all_to_all x5 -> x2, waiting for transfers between devices: 127 us -> 89.6 us  [swap(): lax.all_to_all(value.reshape(experts, cap, -1), 'ep', split_axis=0, conca...]
    all_to_all x5 -> x2, starting transfers between devices: 27 us -> 11 us  [swap(): lax.all_to_all(value.reshape(experts, cap, -1), 'ep', split_axis=0, conca...]
    scatter x3 -> x0, local copies, waits for them, and re-layouts: 15.7 us -> none  [the longest x1 7.21 us: local(): jnp.zeros((slot_room, width), out_grad.dtype).at[destination]]
    gather x3 -> x0, local copies, waits for them, and re-layouts: 6.03 us -> none  [the longest x2 4.09 us: local(): picked_rows = back_rows.reshape(-1, width)[destination]]
    reduce_sum x2 -> x4, other arithmetic: 3.72 us -> 0.88 us  [the longest x1 0.58 us: local(): prob_out = jnp.sum(jnp.where(picks, by_expert[:, None, :], 0.0), axis=2)]
    dot_general x9 -> x12, matrix products: 43.1 us -> 40.7 us  [dot(): return lax.dot_general(a, b, (dims, ((), ())), preferred_element_type=F32)]
  transfers between devices with their start and end apart: 11 -> 8, of which waited for: 3 -> 2; matrix products, arithmetic and copies ran while one was open for 27% -> 14% of each run, Pallas kernels for 0% -> 0%
where the time goes in v1:
time: 224 us; the launch traced here: 223 us
  waiting for transfers between devices  91.8 us (41%)
  blocking collectives  55.6 us (25%)
  matrix products  40.7 us (18%)
  between operations  14.3 us (6%)
  starting transfers between devices  11.7 us (5%)
  local copies, waits for them, and re-layouts  5.35 us (2%)
  other arithmetic  3.67 us (2%)
    all_to_all x2, waiting for transfers between devices, swap(): lax.all_to_all(value.reshape(experts, cap, -1), 'ep', split_axis=0, conca...  89.6 us
    all_to_all x1, blocking collectives, swap(): lax.all_to_all(value.reshape(experts, cap, -1), 'ep', split_axis=0, conca...  55.6 us
    dot_general x12, matrix products, dot(): return lax.dot_general(a, b, (dims, ((), ())), preferred_element_type=F32)  40.7 us
    all_to_all x2, starting transfers between devices, swap(): lax.all_to_all(value.reshape(experts, cap, -1), 'ep', split_axis=0, conca...  11 us
    unnamed x24, local copies, waits for them, and re-layouts  4.84 us
  transfers between devices with their start and end apart: 8, of which 2 were waited for; matrix products, arithmetic and copies ran while one was open for 14% of the time, Pallas kernels for 0%

profile of v1, /device:TPU:0, one launch (start us, length us, event | category | flops | bytes accessed | tf_op | source)
XLA Modules:
  0.0 223.0 jit_solution(6312756498261368295)
XLA Ops:
  7.2 0.7 all-gather.9.cloned.1.call-update
  8.0 0.7 fusion.17
  8.8 0.2 bitcast_compare_fusion
  9.0 2.0 convolution_convert_fusion.3
  11.0 7.4 %all-to-all-start.1 = ((bf16[8,64,2048]{2,1,0:T(8,128)(2,1)}), bf16[8,64,2048]{2,1,0:T(8,128)(2,1)S(1)}, u32[]{:S(2)}, u32[]{:S(2)}) async-start(bf16[8,64,2048]{2,1,0:T(8,128)(2,1)} %bitcast.6), calls=%async_computation.1 | async-start | bytes 4194304 | tf_op jit(solution)/shard_map/all_to_all | solution.py:46
  18.5 0.7 all-gather.7.cloned.1.call-update
  19.2 0.2 select_reduce_fusion.1
  19.5 0.7 convolution_convert_fusion.4
  20.3 1.5 pad_maximum_fusion
  21.8 44.8 %all-to-all-done.1 = bf16[8,64,2048]{2,1,0:T(8,128)(2,1)S(1)} async-done(((bf16[8,64,2048]{2,1,0:T(8,128)(2,1)}), bf16[8,64,2048]{2,1,0:T(8,128)(2,1)S(1)}, u32[]{:S(2)}, u32[]{:S(2)}) %all-to-all-start.1) | async-done | bytes 2097184 | tf_op jit(solution)/shard_map/all_to_all | solution.py:46
  66.7 1.4 copy-done.4
  68.1 3.6 %all-to-all-start = ((bf16[8,64,2176]{2,1,0:T(8,128)(2,1)}), bf16[8,64,2176]{2,1,0:T(8,128)(2,1)S(1)}, u32[]{:S(2)}, u32[]{:S(2)}) async-start(bf16[8,64,2176]{2,1,0:T(8,128)(2,1)} %bitcast.3), calls=%async_computation | async-start | bytes 4456448 | tf_op jit(solution)/shard_map/all_to_all | solution.py:46
  71.8 0.7 all-gather.11.cloned.1.call-update
  72.5 0.2 reduce-scatter.8.cloned.1.call-start
  72.7 5.5 %fusion.6 = f32[512,768]{1,0:T(8,128)} fusion(bf16[512,2048]{1,0:T(8,128)(2,1)} %bitcast.53, bf16[1,2048,768]{2,1,0:T(8,128)(2,1)} %all-gather.9.cloned.1.call-done), kind=kOutput, calls=%fused_computation.10 | convolution fusion | flops 1610612736 | bytes 6815744 | tf_op jit(solution)/shard_map/dot_general | solution.py:12
  78.2 44.8 %all-to-all-done = bf16[8,64,2176]{2,1,0:T(8,128)(2,1)S(1)} async-done(((bf16[8,64,2176]{2,1,0:T(8,128)(2,1)}), bf16[8,64,2176]{2,1,0:T(8,128)(2,1)S(1)}, u32[]{:S(2)}, u32[]{:S(2)}) %all-to-all-start) | async-done | bytes 2228256 | tf_op jit(solution)/shard_map/all_to_all | solution.py:46
  123.1 5.6 %fusion.8 = f32[512,768]{1,0:T(8,128)} fusion(bf16[1,768,2048]{2,1,0:T(8,128)(2,1)} %all-gather.7.cloned.1.call-done, bf16[512,2176]{1,0:T(8,128)(2,1)S(1)} %bitcast.49), kind=kOutput, calls=%fused_computation.12 | convolution fusion | flops 1610612736 | bytes 6815744 | tf_op jit(solution)/shard_map/dot_general | solution.py:12
  128.7 6.1 %multiply_convert_fusion.2 = (bf16[512,768]{1,0:T(8,128)(2,1)S(1)}, bf16[512]{0:T(512)(128)(2,1)S(1)}, bf16[512,768]{1,0:T(8,128)(2,1)S(1)}, bf16[512,768]{1,0:T(8,128)(2,1)S(1)}) fusion(f32[512,768]{1,0:T(8,128)} %fusion.6, f32[512,768]{1,0:T(8,128)} %fusion.8, f32[512]{0:T(512)S(1)} %convert_reduce_fusion.1, bf16[512,2048]{1,0:T(8,128)(2,1)} %bitcast.54, ...), kind=kOutput, calls=%fused_computation.25 | convolution fusion | flops 1618083328 | bytes 10750976 | tf_op jit(solution)/shard_map/dot_general | solution.py:12
  134.8 1.8 fusion
  136.7 0.6 copy-done.8
  137.3 1.8 add_convert_fusion
  139.3 0.2 pad_maximum_fusion.1
  139.5 1.4 copy-done.2
  140.9 3.5 %convolution_convert_fusion = bf16[768,2048]{1,0:T(8,128)(2,1)} fusion(bf16[512,768]{1,0:T(8,128)(2,1)S(1)} %get-tuple-element.12, bf16[512,2176]{1,0:T(8,128)(2,1)S(1)} %bitcast.50), kind=kOutput, calls=%fused_computation.1 | convolution fusion | flops 1612185600 | bytes 6029312 | tf_op jit(solution)/shard_map/dot_general | solution.py:12
  144.5 5.3 %convolution_convert_fusion.1 = bf16[2048,768]{1,0:T(8,128)(2,1)} fusion(bf16[512,2048]{1,0:T(8,128)(2,1)} %bitcast.55, bf16[512,768]{1,0:T(8,128)(2,1)} %copy-done.10), kind=kOutput, calls=%fused_computation.2 | convolution fusion | flops 1612185600 | bytes 6029312 | tf_op jit(solution)/shard_map/dot_general | solution.py:12
  149.8 0.3 reduce-scatter.4.cloned.1.call-start
  150.1 5.4 %convolution_convert_fusion.2 = bf16[2048,768]{1,0:T(8,128)(2,1)} fusion(bf16[512,2048]{1,0:T(8,128)(2,1)} %bitcast.56, bf16[512,768]{1,0:T(8,128)(2,1)} %copy-done.11), kind=kOutput, calls=%fused_computation.3 | convolution fusion | flops 1612185600 | bytes 6029312 | tf_op jit(solution)/shard_map/dot_general | solution.py:12
  155.5 55.6 %all_to_all.15 = bf16[8,64,2176]{2,1,0:T(8,128)(2,1)S(1)} all-to-all(bf16[8,64,2176]{2,1,0:T(8,128)(2,1)S(1)} %bitcast.47), channel_id=1, replica_groups=mesh['groups'=2,'ep'=8,'edp'=2] {'ep'}, dimensions={0} | all-to-all | bytes 4456448 | tf_op jit(solution)/shard_map/all_to_all | solution.py:46
  211.0 1.3 copy-done.3
  212.6 0.1 select_reduce_fusion
  212.7 0.6 select_reduce_fusion.2
  213.3 2.9 %convolution_convert_fusion.5 = bf16[128,2048]{1,0:T(8,128)(2,1)} fusion(pred[512,128]{1,0:T(32,128)(4,1)S(1)} %bitcast_compare_fusion, bf16[512,2176]{1,0:T(8,128)(2,1)} %bitcast.52), kind=kOutput, calls=%fused_computation.16 | convolution fusion | flops 268697600 | bytes 2686976 | tf_op jit(solution)/shard_map/dot_general | solution.py:12
  (43 shorter events, 1.2 us)
Async XLA Ops:
  7.2 1.8 copy-start
  7.2 65.5 %all-gather.9.cloned.1.call-start = ((), (), s32[]{:S(2)}) async-start(), calls=%async_computation.10 | async-start | bytes 4718592 | tf_op jit(solution)/shard_map/all_gather | solution.py:51
  11.0 8.1 %copy-start.6 = (s32[128,2]{0,1:T(2,128)S(1)}, s32[128,2]{0,1:T(2,128)}, u32[]{:S(2)}) copy-start(s32[128,2]{0,1:T(2,128)} %param.9) | copy-start | bytes 3076
  11.0 8.2 %copy-start.7 = (f32[128,2]{0,1:T(2,128)S(1)}, f32[128,2]{0,1:T(2,128)}, u32[]{:S(2)}) copy-start(f32[128,2]{0,1:T(2,128)} %param.10) | copy-start | bytes 3076
  11.0 8.4 %copy-start.5 = (bf16[128,2048]{1,0:T(8,128)(2,1)S(1)}, bf16[128,2048]{1,0:T(8,128)(2,1)}, u32[]{:S(2)}) copy-start(bf16[128,2048]{1,0:T(8,128)(2,1)} %param.8) | copy-start | bytes 1572868
  11.0 55.6 %all-to-all-start.1 = ((bf16[8,64,2048]{2,1,0:T(8,128)(2,1)}), bf16[8,64,2048]{2,1,0:T(8,128)(2,1)S(1)}, u32[]{:S(2)}, u32[]{:S(2)}) async-start(bf16[8,64,2048]{2,1,0:T(8,128)(2,1)} %bitcast.6), calls=%async_computation.1 | async-start | bytes 4194304 | tf_op jit(solution)/shard_map/all_to_all | solution.py:46
  18.4 104.7 %all-gather.7.cloned.1.call-start = ((), (), s32[]{:S(2)}) async-start(), calls=%async_computation.9 | async-start | bytes 4718592 | tf_op jit(solution)/shard_map/all_gather | solution.py:51
  66.7 1.4 copy-start.4
  68.1 54.9 %all-to-all-start = ((bf16[8,64,2176]{2,1,0:T(8,128)(2,1)}), bf16[8,64,2176]{2,1,0:T(8,128)(2,1)S(1)}, u32[]{:S(2)}, u32[]{:S(2)}) async-start(bf16[8,64,2176]{2,1,0:T(8,128)(2,1)} %bitcast.3), calls=%async_computation | async-start | bytes 4456448 | tf_op jit(solution)/shard_map/all_to_all | solution.py:46
  71.8 56.9 %all-gather.11.cloned.1.call-start = ((), (), s32[]{:S(2)}) async-start(), calls=%async_computation.11 | async-start | bytes 4718592 | tf_op jit(solution)/shard_map/all_gather | solution.py:51
  72.5 143.7 %reduce-scatter.8.cloned.1.call-start = ((), (), s32[]{:S(2)}) async-start(), calls=%async_computation.8 | async-start | bytes 4718592 | tf_op jit(solution)/shard_map/reduce_scatter | solution.py:83
  123.0 5.7 %copy-start.1 = (bf16[8,64,2176]{2,1,0:T(8,128)(2,1)}, bf16[8,64,2176]{2,1,0:T(8,128)(2,1)S(1)}, u32[]{:S(2)}) copy-start(bf16[8,64,2176]{2,1,0:T(8,128)(2,1)S(1)} %all-to-all-done) | copy-start | bytes 6684676
  128.7 6.1 %copy-start.9 = (bf16[1,2048,768]{2,1,0:T(8,128)(2,1)S(1)}, bf16[1,2048,768]{2,1,0:T(8,128)(2,1)}, u32[]{:S(2)}) copy-start(bf16[1,2048,768]{2,1,0:T(8,128)(2,1)} %all-gather.11.cloned.1.call-done) | copy-start | bytes 9437188
  134.8 1.9 copy-start.11
  134.8 1.9 copy-start.10
  134.8 2.4 %copy-start.8 = (bf16[1,2048,768]{2,1,0:T(8,128)(2,1)S(1)}, bf16[1,2048,768]{2,1,0:T(8,128)(2,1)}, u32[]{:S(2)}) copy-start(bf16[1,2048,768]{2,1,0:T(8,128)(2,1)} %all-gather.9.cloned.1.call-done) | copy-start | bytes 9437188
  139.3 1.6 copy-start.2
  144.5 71.7 %reduce-scatter.6.cloned.1.call-start = ((), (), s32[]{:S(2)}) async-start(), calls=%async_computation.7 | async-start | bytes 4718592 | tf_op jit(solution)/shard_map/reduce_scatter | solution.py:83
  149.8 66.4 %reduce-scatter.4.cloned.1.call-start = ((), (), s32[]{:S(2)}) async-start(), calls=%async_computation.6 | async-start | bytes 4718592 | tf_op jit(solution)/shard_map/reduce_scatter | solution.py:83
  211.0 1.3 copy-start.3
Sparse Core Ops, SparseCore 0:
  9.6 14.8 all-gather.8
  26.0 13.2 all-gather.6
  74.1 13.5 all-gather.10
  144.6 9.9 reduce-scatter.7
  157.3 12.0 reduce-scatter.5
  172.1 12.0 reduce-scatter.3

commit v2 on v1

--- a/solution.py
+++ b/solution.py
@@ -1,6 +1,10 @@
+import functools
+
 import jax
 import jax.numpy as jnp
 from jax import lax
+from jax.experimental import pallas as pl
+from jax.experimental.pallas import tpu as pltpu
 from jax.sharding import PartitionSpec as P
 
 F32 = jnp.float32
@@ -12,7 +16,7 @@
     return lax.dot_general(a, b, (dims, ((), ())), preferred_element_type=F32)
 
 
-def routing(routes, probs, experts, cap):
+def routing(routes, probs, experts):
     tok, top = routes.shape
     picks = routes[:, :, None] == jnp.arange(experts, dtype=jnp.int32)[None, None, :]
     chosen = jnp.any(picks, axis=1)
@@ -21,19 +25,19 @@
     earlier = (order[:, None] > order[None, :]).astype(BF16)
     place = dot(earlier, chosen.astype(BF16), ((1,), (0,))).astype(jnp.int32)
     place = jnp.where(chosen, place, -1)
-    slot = jnp.arange(cap, dtype=jnp.int32)
-    select = place.T[:, None, :] == slot[None, :, None]
-    return picks, select, weight
-
-
-def local(hidden_in, out_grad, routes, probs, w_gate, w_up, w_down):
+    return picks, place, weight
+
+
+def general(hidden_in, out_grad, routes, probs, w_gate, w_up, w_down):
     tok, top = routes.shape
     width = hidden_in.shape[1]
     ep = lax.axis_size("ep")
     experts = ep * w_gate.shape[0]
     cap = max(8, 2 * tok * top // experts)
     rows = experts * cap
-    picks, select, weight = routing(routes, probs, experts, cap)
+    picks, place, weight = routing(routes, probs, experts)
+    slot = jnp.arange(cap, dtype=jnp.int32)
+    select = place.T[:, None, :] == slot[None, :, None]
     select_rows = select.reshape(rows, tok).astype(BF16)
     row_weight = jnp.sum(jnp.where(select, weight.T[:, None, :], 0.0), axis=2).reshape(rows, 1)
     send_in = dot(select_rows, hidden_in, ((1,), (0,))).astype(BF16)
@@ -91,6 +95,284 @@
     )
 
 
+def partner(me, bits, d):
+    total = 0
+    for i in range(bits):
+        bit = lax.rem(me // (1 << i), 2)
+        total = total + (1 - bit if (d >> i) & 1 else bit) * (1 << i)
+    return total
+
+
+def kernel(ep, piece, hidden, grad, select, select_t, weight, wg, wu, wd,
+           in_out, prob_out, gw, uw, dw,
+           send_in, send_grad, rows_in, rows_grad, send_back, back,
+           gate_full, up_full, down_full, active, upper, slope,
+           gate_grad, up_grad, scaled, gate_send, up_send, down_send,
+           gate_got, up_got, down_got,
+           row_send, row_recv, own_sem, w_send, w_recv, w_own, g_send, g_recv):
+    me, side = lax.axis_index("ep"), lax.axis_index("edp")
+    other = 1 - side
+    bits = ep.bit_length() - 1
+    width, ff = hidden.shape[1], wg.shape[1]
+    part_rows = ep * piece
+    half, down_half = width // 2, ff // 2
+    partners = [(d, partner(me, bits, d)) for d in range(ep - 1, 0, -1)]
+
+    barrier = pltpu.get_barrier_semaphore()
+    for d, target in partners:
+        pl.semaphore_signal(barrier, inc=1, device_id={"ep": target})
+    pl.semaphore_signal(barrier, inc=1, device_id={"edp": other})
+
+    def row_slice(part, owner):
+        return pl.ds(pl.multiple_of(part * part_rows + owner * piece, piece), piece)
+
+    def dispatch(part, source, sink):
+        rows = pl.ds(part * part_rows, part_rows)
+
+        def tile(c, carry):
+            cols = pl.ds(pl.multiple_of(c * 512, 512), 512)
+            sink[rows, cols] = dot(select[rows, :], source[:, cols], ((1,), (0,))).astype(BF16)
+            return carry
+
+        lax.fori_loop(0, width // 512, tile, 0)
+
+    def spread(kind, part, source, sink):
+        copies = []
+        for d, target in partners:
+            copies.append(pltpu.make_async_remote_copy(
+                src_ref=source.at[row_slice(part, target)],
+                dst_ref=sink.at[row_slice(part, me)],
+                send_sem=row_send.at[kind, part, d],
+                recv_sem=row_recv.at[kind, part, d],
+                device_id={"ep": target},
+            ))
+        for copy in copies:
+            copy.start()
+        own = pltpu.make_async_copy(
+            source.at[row_slice(part, me)], sink.at[row_slice(part, me)], own_sem.at[kind, part])
+        own.start()
+        return copies, own
+
+    def arrive(group):
+        copies, own = group
+        own.wait()
+        for copy in copies:
+            copy.wait_recv()
+
+    dispatch(0, hidden, send_in)
+    pl.semaphore_wait(barrier, ep)
+    in0 = spread(0, 0, send_in, rows_in)
+    dispatch(0, grad, send_grad)
+    send_grad[:, pl.ds(width, LANE)] = weight[...]
+    grad0 = spread(1, 0, send_grad, rows_grad)
+
+    exchanged = []
+    for i, (ref, full) in enumerate(((wg, gate_full), (wu, up_full), (wd, down_full))):
+        depth = ref.shape[0]
+        place = pl.ds(pl.multiple_of(side * depth, depth), depth)
+        copy = pltpu.make_async_remote_copy(
+            src_ref=ref, dst_ref=full.at[place], send_sem=w_send.at[i], recv_sem=w_recv.at[i],
+            device_id={"edp": other})
+        copy.start()
+        own = pltpu.make_async_copy(ref, full.at[place], w_own.at[i])
+        own.start()
+        exchanged.append((copy, own))
+
+    dispatch(1, hidden, send_in)
+    in1 = spread(0, 1, send_in, rows_in)
+    dispatch(1, grad, send_grad)
+    grad1 = spread(1, 1, send_grad, rows_grad)
+
+    for copy, own in exchanged:
+        own.wait()
+        copy.wait_recv()
+
+    def forward(part):
+        rows = pl.ds(part * part_rows, part_rows)
+
+        def tile(c, carry):
+            cols = pl.ds(pl.multiple_of(c * 256, 256), 256)
+            x = rows_in[rows, :]
+            gate = dot(x, gate_full[:, cols], ((1,), (0,)))
+            up = dot(x, up_full[:, cols], ((1,), (0,)))
+            sigma = jax.nn.sigmoid(gate)
+            active[:, cols] = gate * sigma
+            upper[:, cols] = up
+            slope[:, cols] = up * sigma * (1.0 + gate * (1.0 - sigma))
+            return carry
+
+        lax.fori_loop(0, ff // 256, tile, 0)
+
+    def backward(part):
+        rows = pl.ds(part * part_rows, part_rows)
+        p = rows_grad[rows, pl.ds(width, LANE)].astype(F32)[:, :1]
+
+        def tile(c, total):
+            cols = pl.ds(pl.multiple_of(c * 256, 256), 256)
+            plain = dot(rows_grad[rows, pl.ds(0, width)], down_full[cols, :], ((1,), (1,)))
+            act = active[:, cols]
+            hid = act * upper[:, cols]
+            hidden_grad = plain * p
+            up_grad[rows, cols] = (hidden_grad * act).astype(BF16)
+            gate_grad[rows, cols] = (hidden_grad * slope[:, cols]).astype(BF16)
+            scaled[rows, cols] = (hid * p).astype(BF16)
+            return total + jnp.sum(hid * plain, axis=1, keepdims=True)
+
+        total = lax.fori_loop(0, ff // 256, tile, jnp.zeros((part_rows, 1), F32))
+        send_back[rows, pl.ds(width, LANE)] = jnp.broadcast_to(total, (part_rows, LANE)).astype(BF16)
+
+        def out_tile(c, carry):
+            cols = pl.ds(pl.multiple_of(c * 256, 256), 256)
+            value = dot(gate_grad[rows, :], gate_full[cols, :], ((1,), (1,)))
+            value = value + dot(up_grad[rows, :], up_full[cols, :], ((1,), (1,)))
+            send_back[rows, cols] = value.astype(BF16)
+            return carry
+
+        lax.fori_loop(0, width // 256, out_tile, 0)
+
+    arrive(in0)
+    forward(0)
+    arrive(grad0)
+    backward(0)
+    back0 = spread(2, 0, send_back, back)
+    arrive(in1)
+    forward(1)
+    arrive(grad1)
+    backward(1)
+    back1 = spread(2, 1, send_back, back)
+
+    def wide(which, sink, factor):
+        def tile(c, carry):
+            at = pl.ds(pl.multiple_of(which * half + c * 256, 256), 256)
+            value = dot(rows_in[:, at], factor[...], ((0,), (0,)))
+            sink[pl.ds(pl.multiple_of(c * 256, 256), 256), :] = value.astype(BF16)
+            return carry
+
+        lax.fori_loop(0, half // 256, tile, 0)
+
+    def tall(which, sink):
+        lhs = pl.ds(pl.multiple_of(which * down_half, LANE), down_half)
+
+        def tile(c, carry):
+            cols = pl.ds(pl.multiple_of(c * 512, 512), 512)
+            sink[:, cols] = dot(scaled[:, lhs], rows_grad[:, cols], ((0,), (0,))).astype(BF16)
+            return carry
+
+        lax.fori_loop(0, width // 512, tile, 0)
+
+    def pass_on(i, source, sink):
+        copy = pltpu.make_async_remote_copy(
+            src_ref=source, dst_ref=sink, send_sem=g_send.at[i], recv_sem=g_recv.at[i],
+            device_id={"edp": other})
+        copy.start()
+        return copy
+
+    wide(other, gate_send, gate_grad)
+    passed = [pass_on(0, gate_send, gate_got)]
+    wide(other, up_send, up_grad)
+    passed.append(pass_on(1, up_send, up_got))
+    tall(other, down_send)
+    passed.append(pass_on(2, down_send, down_got))
+    wide(side, gw, gate_grad)
+    wide(side, uw, up_grad)
+    tall(side, dw)
+    for copy, got, sink in zip(passed, (gate_got, up_got, down_got), (gw, uw, dw)):
+        copy.wait_recv()
+        steps = sink.shape[0] // 128
+
+        def add(r, carry, got=got, sink=sink):
+            at = pl.ds(pl.multiple_of(r * 128, 128), 128)
+            sink[at, :] = (sink[at, :].astype(F32) + got[at, :].astype(F32)).astype(BF16)
+            return carry
+
+        lax.fori_loop(0, steps, add, 0)
+
+    arrive(back0)
+    arrive(back1)
+
+    def combine(c, carry):
+        cols = pl.ds(pl.multiple_of(c * 512, 512), 512)
+        in_out[:, cols] = dot(select_t[...], back[:, cols], ((1,), (0,))).astype(BF16)
+        return carry
+
+    lax.fori_loop(0, width // 512, combine, 0)
+    prob_out[...] = back[:, pl.ds(width, LANE)]
+    for copies, own in (in0, grad0, in1, grad1, back0, back1):
+        for copy in copies:
+            copy.wait_send()
+    for copy, own in exchanged:
+        copy.wait_send()
+    for copy in passed:
+        copy.wait_send()
+
+
+def fused(hidden_in, out_grad, routes, probs, w_gate, w_up, w_down):
+    tok, top = routes.shape
+    width = hidden_in.shape[1]
+    ep = lax.axis_size("ep")
+    ff = w_gate.shape[2]
+    cap = 2 * tok * top // ep
+    piece = cap // 2
+    rows = ep * cap
+    picks, place, weight = routing(routes, probs, ep)
+    slot = jnp.arange(cap, dtype=jnp.int32).reshape(2, 1, piece, 1)
+    select = place.T[None, :, None, :] == slot
+    row_weight = jnp.sum(jnp.where(select, weight.T[None, :, None, :], 0.0), axis=3)
+    row_weight = jnp.broadcast_to(row_weight.reshape(rows, 1).astype(BF16), (rows, LANE))
+    select_rows = select.reshape(rows, tok).astype(BF16)
+    vmem = pl.BlockSpec(memory_space=pltpu.VMEM)
+    hbm = pl.BlockSpec(memory_space=pl.ANY)
+
+    def buf(*shape, dtype=BF16):
+        return pltpu.VMEM(shape, dtype)
+
+    wide, down = (width // 2, ff), (ff // 2, width)
+    dma = pltpu.SemaphoreType.DMA
+    input_grad, back_prob, gw, uw, dw = pl.pallas_call(
+        functools.partial(kernel, ep, piece),
+        out_shape=(
+            jax.ShapeDtypeStruct((tok, width), BF16),
+            jax.ShapeDtypeStruct((rows, LANE), BF16),
+            jax.ShapeDtypeStruct(wide, BF16),
+            jax.ShapeDtypeStruct(wide, BF16),
+            jax.ShapeDtypeStruct(down, BF16),
+        ),
+        in_specs=[vmem] * 5 + [hbm] * 3,
+        out_specs=(vmem,) * 5,
+        scratch_shapes=[
+            buf(rows, width), buf(rows, width + LANE), buf(rows, width), buf(rows, width + LANE),
+            buf(rows, width + LANE), buf(rows, width + LANE),
+            buf(width, ff), buf(width, ff), buf(ff, width),
+            buf(rows // 2, ff, dtype=F32), buf(rows // 2, ff, dtype=F32), buf(rows // 2, ff, dtype=F32),
+            buf(rows, ff), buf(rows, ff), buf(rows, ff),
+            buf(*wide), buf(*wide), buf(*down), buf(*wide), buf(*wide), buf(*down),
+            dma((3, 2, ep)), dma((3, 2, ep)), dma((3, 2)),
+            dma((3,)), dma((3,)), dma((3,)), dma((3,)), dma((3,)),
+        ],
+        compiler_params=pltpu.CompilerParams(
+            collective_id=0, has_side_effects=True, vmem_limit_bytes=60 << 20
+        ),
+        cost_estimate=pl.CostEstimate(
+            flops=16 * rows * width * ff, bytes_accessed=24 * rows * width, transcendentals=rows * ff
+        ),
+    )(hidden_in, out_grad, select_rows, select_rows.T, row_weight, w_gate[0], w_up[0], w_down[0])
+    back_prob = back_prob[:, 0].astype(F32).reshape(2, ep, piece, 1)
+    by_expert = jnp.sum(jnp.where(select, back_prob, 0.0), axis=(0, 2)).T
+    prob_grad = jnp.sum(jnp.where(picks, by_expert[:, None, :], 0.0), axis=2)
+    return input_grad, prob_grad, gw[None], uw[None], dw[None]
+
+
+def local(*arrays):
+    tok, top = arrays[2].shape
+    width, ff = arrays[4].shape[1] * 2, arrays[4].shape[2]
+    ep = lax.axis_size("ep")
+    whole_tiles = tok % 128 == 0 and width % 512 == 0 and ff % 256 == 0
+    one_each = arrays[4].shape[0] == 1 and lax.axis_size("edp") == 2
+    if one_each and whole_tiles and ep <= 8 and ep & (ep - 1) == 0 and 2 * tok * top // ep % 64 == 0:
+        return fused(*arrays)
+    return general(*arrays)
+
+
 def solution(mesh):
     tokens = P(("groups", "ep", "edp"), None)
     weights = P("ep", "edp", None)

time: 224 us -> 169 us (0.75)
  Pallas kernels: 0 us -> 154 us
  waiting for transfers between devices: 91.8 us -> 0 us
  blocking collectives: 55.6 us -> 0 us
  matrix products: 40.7 us -> 0.14 us
  between operations: 14.3 us -> 0.69 us
  starting transfers between devices: 11.7 us -> 0 us
  local copies, waits for them, and re-layouts: 5.35 us -> 9.73 us
    pallas_call x0 -> x1, Pallas kernels: none -> 154 us  [fused(): pl.pallas_call(functools.partial(kernel, ep, piece), out_shape=(jax.Shape...]
    all_to_all x2 -> x0, waiting for transfers between devices: 89.6 us -> none  [swap(): lax.all_to_all(value.reshape(experts, cap, -1), 'ep', split_axis=0, conca...]
    all_to_all x1 -> x0, blocking collectives: 55.6 us -> none  [swap(): lax.all_to_all(value.reshape(experts, cap, -1), 'ep', split_axis=0, conca...]
    dot_general x12 -> x1, matrix products: 40.7 us -> 0.14 us  [dot(): return lax.dot_general(a, b, (dims, ((), ())), preferred_element_type=F32)]
    all_to_all x2 -> x0, starting transfers between devices: 11 us -> none  [swap(): lax.all_to_all(value.reshape(experts, cap, -1), 'ep', split_axis=0, conca...]
    unnamed x24 -> x10, local copies, waits for them, and re-layouts: 4.84 us -> 7.77 us
  transfers between devices with their start and end apart: 8 -> 0, of which waited for: 2 -> 0; matrix products, arithmetic and copies ran while one was open for 14% -> 0% of each run, Pallas kernels for 0% -> 0%
where the time goes in v2:
time: 169 us
  Pallas kernels  154 us (91%)
  local copies, waits for them, and re-layouts  9.73 us (6%)
  other arithmetic  4.09 us (2%)
    pallas_call x1, Pallas kernels, fused(): pl.pallas_call(functools.partial(kernel, ep, piece), out_shape=(jax.Shape...  154 us
    unnamed x10, local copies, waits for them, and re-layouts  7.77 us

profile of v2, /device:TPU:0, one launch (start us, length us, event | category | flops | bytes accessed | tf_op | source)
XLA Modules:
  0.0 168.7 jit_solution(689708451257295740)
XLA Ops:
  0.6 0.7 fusion.3
  1.3 0.1 fusion
  1.5 0.7 select_reduce_fusion.1
  2.2 0.2 fusion.1
  2.4 0.1 convert_element_type.33
  2.5 0.1 eq.43
  2.6 0.8 broadcast_in_dim.75.weight
  3.4 0.1 copy.25
  3.5 0.7 fusion.5.select_t
  4.2 0.8 copy.26.select
  5.0 0.0 copy-start.2
  5.0 154.1 %shard_map.110 = (bf16[128,2048]{1,0:T(8,128)(2,1)}, bf16[512,128]{1,0:T(8,128)(2,1)}, bf16[1024,768]{1,0:T(8,128)(2,1)}, bf16[1024,768]{1,0:T(8,128)(2,1)}, bf16[384,2048]{1,0:T(8,128)(2,1)}) custom-call(bf16[128,2048]{1,0:T(8,128)(2,1)} %hidden.1, bf16[128,2048]{1,0:T(8,128)(2,1)} %grad.1, bf16[512,128]{1,0:T(8,128)(2,1)} %copy.26.select, ...), custom_call_target="tpu_custom_call" | custom-call | flops 12884901888 | bytes 25165824 | tf_op jit(solution)/shard_map/pallas_call | solution.py:331
  159.1 1.0 convert_reduce_fusion
  160.1 0.1 reshape.62
  160.2 0.2 fusion.2
  160.3 0.0 copy-done.2
  160.3 0.6 select_reduce_fusion
  160.9 1.9 %copy.31 = bf16[128,2048]{1,0:T(8,128)(2,1)} copy(bf16[128,2048]{1,0:T(8,128)(2,1)} %get-tuple-element.20) | data formatting | bytes 1048576
  162.8 0.0 copy-start.1
  162.8 2.8 %copy.32 = bf16[1,1024,768]{2,1,0:T(8,128)(2,1)} copy(bf16[1,1024,768]{2,1,0:T(8,128)(2,1)} %bitcast.16) | data formatting | bytes 3145728
  165.6 0.0 copy-done.1
  165.6 0.0 copy-start
  165.6 1.1 copy.33
  166.7 0.8 copy-done
  167.6 1.1 copy.34
  (4 shorter events, 0.1 us)
Async XLA Ops:
  5.0 155.3 %copy-start.2 = (s32[128,2]{0,1:T(2,128)S(1)}, s32[128,2]{0,1:T(2,128)}, u32[]{:S(2)}) copy-start(s32[128,2]{0,1:T(2,128)} %param.9) | copy-start | bytes 3076
  162.8 2.8 %copy-start.1 = (bf16[1024,768]{1,0:T(8,128)(2,1)S(1)}, bf16[1024,768]{1,0:T(8,128)(2,1)}, u32[]{:S(2)}) copy-start(bf16[1024,768]{1,0:T(8,128)(2,1)} %get-tuple-element.13) | copy-start | bytes 4718596
  165.6 2.0 %copy-start = (bf16[384,2048]{1,0:T(8,128)(2,1)S(1)}, bf16[384,2048]{1,0:T(8,128)(2,1)}, u32[]{:S(2)}) copy-start(bf16[384,2048]{1,0:T(8,128)(2,1)} %get-tuple-element.14) | copy-start | bytes 4718596

commit v3 on v2

--- a/solution.py
+++ b/solution.py
@@ -103,28 +103,42 @@
     return total
 
 
-def kernel(ep, piece, hidden, grad, select, select_t, weight, wg, wu, wd,
+def kernel(quad, cap, hidden, grad, table, wg, wu, wd,
            in_out, prob_out, gw, uw, dw,
            send_in, send_grad, rows_in, rows_grad, send_back, back,
            gate_full, up_full, down_full, active, upper, slope,
            gate_grad, up_grad, scaled, gate_send, up_send, down_send,
            gate_got, up_got, down_got,
-           row_send, row_recv, own_sem, w_send, w_recv, w_own, g_send, g_recv):
+           far_table, far_hidden, far_grad, select, relay_in, far_in, relay_prob, far_prob,
+           row_send, row_recv, own_sem, w_send, w_recv, w_own, g_send, g_recv, m_send, m_recv):
     me, side = lax.axis_index("ep"), lax.axis_index("edp")
     other = 1 - side
-    bits = ep.bit_length() - 1
+    team, seat = me // quad, lax.rem(me, quad)
+    mirror = (1 - team) * quad + seat
+    bits = quad.bit_length() - 1
     width, ff = hidden.shape[1], wg.shape[1]
-    part_rows = ep * piece
+    tok = hidden.shape[0]
+    part_rows = quad * cap
     half, down_half = width // 2, ff // 2
-    partners = [(d, partner(me, bits, d)) for d in range(ep - 1, 0, -1)]
+    partners = [(d, partner(seat, bits, d)) for d in range(quad - 1, 0, -1)]
 
     barrier = pltpu.get_barrier_semaphore()
     for d, target in partners:
-        pl.semaphore_signal(barrier, inc=1, device_id={"ep": target})
+        pl.semaphore_signal(barrier, inc=1, device_id={"ep": team * quad + target})
+    pl.semaphore_signal(barrier, inc=1, device_id={"ep": mirror})
     pl.semaphore_signal(barrier, inc=1, device_id={"edp": other})
 
     def row_slice(part, owner):
-        return pl.ds(pl.multiple_of(part * part_rows + owner * piece, piece), piece)
+        return pl.ds(pl.multiple_of(part * part_rows + owner * cap, cap), cap)
+
+    def choose(part, entry):
+        slot = lax.broadcasted_iota(jnp.int32, (cap, tok), 0).astype(F32)
+        for q in range(quad):
+            rows = pl.ds(part * part_rows + q * cap, cap)
+            mask = entry[q : q + 1, :] == slot
+            select[rows, :] = jnp.where(mask, 1.0, 0.0).astype(BF16)
+            w = jnp.sum(jnp.where(mask, entry[quad + q : quad + q + 1, :], 0.0), axis=1, keepdims=True)
+            send_grad[rows, pl.ds(width, LANE)] = jnp.broadcast_to(w, (cap, LANE)).astype(BF16)
 
     def dispatch(part, source, sink):
         rows = pl.ds(part * part_rows, part_rows)
@@ -136,20 +150,22 @@
 
         lax.fori_loop(0, width // 512, tile, 0)
 
-    def spread(kind, part, source, sink):
+    def spread(kind, part, source, sink, low, size):
+        cols = pl.ds(low, size)
         copies = []
         for d, target in partners:
             copies.append(pltpu.make_async_remote_copy(
-                src_ref=source.at[row_slice(part, target)],
-                dst_ref=sink.at[row_slice(part, me)],
+                src_ref=source.at[row_slice(part, target), cols],
+                dst_ref=sink.at[row_slice(part, seat), cols],
                 send_sem=row_send.at[kind, part, d],
                 recv_sem=row_recv.at[kind, part, d],
-                device_id={"ep": target},
+                device_id={"ep": team * quad + target},
             ))
         for copy in copies:
             copy.start()
         own = pltpu.make_async_copy(
-            source.at[row_slice(part, me)], sink.at[row_slice(part, me)], own_sem.at[kind, part])
+            source.at[row_slice(part, seat), cols], sink.at[row_slice(part, seat), cols],
+            own_sem.at[kind, part])
         own.start()
         return copies, own
 
@@ -159,12 +175,21 @@
         for copy in copies:
             copy.wait_recv()
 
+    def cross(i, source, sink):
+        copy = pltpu.make_async_remote_copy(
+            src_ref=source, dst_ref=sink, send_sem=m_send.at[i], recv_sem=m_recv.at[i],
+            device_id={"ep": mirror})
+        copy.start()
+        return copy
+
+    choose(0, table[team])
     dispatch(0, hidden, send_in)
-    pl.semaphore_wait(barrier, ep)
-    in0 = spread(0, 0, send_in, rows_in)
+    pl.semaphore_wait(barrier, quad + 1)
+    crossed = [cross(0, table.at[1 - team], far_table), cross(1, hidden, far_hidden)]
+    in0 = spread(0, 0, send_in, rows_in, 0, width)
+    crossed.append(cross(2, grad, far_grad))
     dispatch(0, grad, send_grad)
-    send_grad[:, pl.ds(width, LANE)] = weight[...]
-    grad0 = spread(1, 0, send_grad, rows_grad)
+    grad0 = spread(1, 0, send_grad, rows_grad, 0, width + LANE)
 
     exchanged = []
     for i, (ref, full) in enumerate(((wg, gate_full), (wu, up_full), (wd, down_full))):
@@ -178,11 +203,11 @@
         own.start()
         exchanged.append((copy, own))
 
-    dispatch(1, hidden, send_in)
-    in1 = spread(0, 1, send_in, rows_in)
-    dispatch(1, grad, send_grad)
-    grad1 = spread(1, 1, send_grad, rows_grad)
-
+    crossed[0].wait_recv()
+    choose(1, far_table[...])
+    crossed[1].wait_recv()
+    dispatch(1, far_hidden, send_in)
+    in1 = spread(0, 1, send_in, rows_in, 0, width)
     for copy, own in exchanged:
         own.wait()
         copy.wait_recv()
@@ -221,6 +246,9 @@
         total = lax.fori_loop(0, ff // 256, tile, jnp.zeros((part_rows, 1), F32))
         send_back[rows, pl.ds(width, LANE)] = jnp.broadcast_to(total, (part_rows, LANE)).astype(BF16)
 
+    def returns(part, kind, low, size):
+        rows = pl.ds(part * part_rows, part_rows)
+
         def out_tile(c, carry):
             cols = pl.ds(pl.multiple_of(c * 256, 256), 256)
             value = dot(gate_grad[rows, :], gate_full[cols, :], ((1,), (1,)))
@@ -228,18 +256,23 @@
             send_back[rows, cols] = value.astype(BF16)
             return carry
 
-        lax.fori_loop(0, width // 256, out_tile, 0)
+        lax.fori_loop(low // 256, (low + size) // 256, out_tile, 0)
+        tail = LANE if low + size == width else 0
+        return spread(kind, part, send_back, back, low, size + tail)
 
     arrive(in0)
     forward(0)
+    crossed[2].wait_recv()
+    dispatch(1, far_grad, send_grad)
+    grad1 = spread(1, 1, send_grad, rows_grad, 0, width + LANE)
     arrive(grad0)
     backward(0)
-    back0 = spread(2, 0, send_back, back)
+    back0 = returns(0, 2, 0, width)
     arrive(in1)
     forward(1)
     arrive(grad1)
     backward(1)
-    back1 = spread(2, 1, send_back, back)
+    back1 = [returns(1, 2, 0, half), returns(1, 3, half, half)]
 
     def wide(which, sink, factor):
         def tile(c, carry):
@@ -273,6 +306,35 @@
     passed.append(pass_on(1, up_send, up_got))
     tall(other, down_send)
     passed.append(pass_on(2, down_send, down_got))
+
+    def combine(part, sink, low, size, extra=None):
+        rows = pl.ds(part * part_rows, part_rows)
+
+        def tile(c, carry):
+            cols = pl.ds(pl.multiple_of(c * 512, 512), 512)
+            value = dot(select[rows, :], back[rows, cols], ((0,), (0,)))
+            if extra is not None:
+                value = value + extra[:, cols].astype(F32)
+            sink[:, cols] = value.astype(BF16)
+            return carry
+
+        lax.fori_loop(low // 512, (low + size) // 512, tile, 0)
+
+    def prob_table(part):
+        lines = []
+        for q in range(quad):
+            rows = pl.ds(part * part_rows + q * cap, cap)
+            value = select[rows, :].astype(F32) * back[rows, pl.ds(width, LANE)].astype(F32)
+            lines.append(jnp.sum(value, axis=0, keepdims=True))
+        return jnp.concatenate(lines + lines, axis=0)
+
+    for i, group in enumerate(back1):
+        arrive(group)
+        combine(1, relay_in, i * half, half)
+        cols = pl.ds(i * half, half)
+        crossed.append(cross(3 + i, relay_in.at[:, cols], far_in.at[:, cols]))
+    relay_prob[...] = prob_table(1)
+    crossed.append(cross(5, relay_prob, far_prob))
     wide(side, gw, gate_grad)
     wide(side, uw, up_grad)
     tall(side, dw)
@@ -288,18 +350,17 @@
         lax.fori_loop(0, steps, add, 0)
 
     arrive(back0)
-    arrive(back1)
-
-    def combine(c, carry):
-        cols = pl.ds(pl.multiple_of(c * 512, 512), 512)
-        in_out[:, cols] = dot(select_t[...], back[:, cols], ((1,), (0,))).astype(BF16)
-        return carry
-
-    lax.fori_loop(0, width // 512, combine, 0)
-    prob_out[...] = back[:, pl.ds(width, LANE)]
-    for copies, own in (in0, grad0, in1, grad1, back0, back1):
+    prob_out[team] = prob_table(0)
+    for i in range(2):
+        crossed[3 + i].wait_recv()
+        combine(0, in_out, i * half, half, far_in)
+    crossed[5].wait_recv()
+    prob_out[1 - team] = far_prob[...]
+    for copies, own in (in0, grad0, in1, grad1, back0, back1[0], back1[1]):
         for copy in copies:
             copy.wait_send()
+    for copy in crossed:
+        copy.wait_send()
     for copy, own in exchanged:
         copy.wait_send()
     for copy in passed:
@@ -312,14 +373,12 @@
     ep = lax.axis_size("ep")
     ff = w_gate.shape[2]
     cap = 2 * tok * top // ep
-    piece = cap // 2
+    quad = ep // 2
     rows = ep * cap
     picks, place, weight = routing(routes, probs, ep)
-    slot = jnp.arange(cap, dtype=jnp.int32).reshape(2, 1, piece, 1)
-    select = place.T[None, :, None, :] == slot
-    row_weight = jnp.sum(jnp.where(select, weight.T[None, :, None, :], 0.0), axis=3)
-    row_weight = jnp.broadcast_to(row_weight.reshape(rows, 1).astype(BF16), (rows, LANE))
-    select_rows = select.reshape(rows, tok).astype(BF16)
+    table = jnp.concatenate(
+        [place.T.astype(F32).reshape(2, quad, tok), weight.T.reshape(2, quad, tok)], axis=1
+    )
     vmem = pl.BlockSpec(memory_space=pltpu.VMEM)
     hbm = pl.BlockSpec(memory_space=pl.ANY)
 
@@ -329,15 +388,15 @@
     wide, down = (width // 2, ff), (ff // 2, width)
     dma = pltpu.SemaphoreType.DMA
     input_grad, back_prob, gw, uw, dw = pl.pallas_call(
-        functools.partial(kernel, ep, piece),
+        functools.partial(kernel, quad, cap),
         out_shape=(
             jax.ShapeDtypeStruct((tok, width), BF16),
-            jax.ShapeDtypeStruct((rows, LANE), BF16),
+            jax.ShapeDtypeStruct((2, ep, tok), F32),
             jax.ShapeDtypeStruct(wide, BF16),
             jax.ShapeDtypeStruct(wide, BF16),
             jax.ShapeDtypeStruct(down, BF16),
         ),
-        in_specs=[vmem] * 5 + [hbm] * 3,
+        in_specs=[vmem] * 3 + [hbm] * 3,
         out_specs=(vmem,) * 5,
         scratch_shapes=[
             buf(rows, width), buf(rows, width + LANE), buf(rows, width), buf(rows, width + LANE),
@@ -346,8 +405,10 @@
             buf(rows // 2, ff, dtype=F32), buf(rows // 2, ff, dtype=F32), buf(rows // 2, ff, dtype=F32),
             buf(rows, ff), buf(rows, ff), buf(rows, ff),
             buf(*wide), buf(*wide), buf(*down), buf(*wide), buf(*wide), buf(*down),
-            dma((3, 2, ep)), dma((3, 2, ep)), dma((3, 2)),
-            dma((3,)), dma((3,)), dma((3,)), dma((3,)), dma((3,)),
+            buf(ep, tok, dtype=F32), buf(tok, width), buf(tok, width), buf(rows, tok),
+            buf(tok, width), buf(tok, width), buf(ep, tok, dtype=F32), buf(ep, tok, dtype=F32),
+            dma((4, 2, quad)), dma((4, 2, quad)), dma((4, 2)),
+            dma((3,)), dma((3,)), dma((3,)), dma((3,)), dma((3,)), dma((6,)), dma((6,)),
         ],
         compiler_params=pltpu.CompilerParams(
             collective_id=0, has_side_effects=True, vmem_limit_bytes=60 << 20
@@ -355,9 +416,8 @@
         cost_estimate=pl.CostEstimate(
             flops=16 * rows * width * ff, bytes_accessed=24 * rows * width, transcendentals=rows * ff
         ),
-    )(hidden_in, out_grad, select_rows, select_rows.T, row_weight, w_gate[0], w_up[0], w_down[0])
-    back_prob = back_prob[:, 0].astype(F32).reshape(2, ep, piece, 1)
-    by_expert = jnp.sum(jnp.where(select, back_prob, 0.0), axis=(0, 2)).T
+    )(hidden_in, out_grad, table, w_gate[0], w_up[0], w_down[0])
+    by_expert = back_prob[:, :quad].reshape(ep, tok).T
     prob_grad = jnp.sum(jnp.where(picks, by_expert[:, None, :], 0.0), axis=2)
     return input_grad, prob_grad, gw[None], uw[None], dw[None]
 
@@ -368,7 +428,7 @@
     ep = lax.axis_size("ep")
     whole_tiles = tok % 128 == 0 and width % 512 == 0 and ff % 256 == 0
     one_each = arrays[4].shape[0] == 1 and lax.axis_size("edp") == 2
-    if one_each and whole_tiles and ep <= 8 and ep & (ep - 1) == 0 and 2 * tok * top // ep % 64 == 0:
+    if one_each and whole_tiles and ep == 8 and tok == LANE and 2 * tok * top // ep % 32 == 0:
         return fused(*arrays)
     return general(*arrays)
 

time: 169 us -> 134 us (0.79)
  Pallas kernels: 154 us -> 122 us
    pallas_call x1, Pallas kernels: 154 us -> 122 us  [fused(): pl.pallas_call(functools.partial(kernel, quad, cap), out_shape=(jax.Shape...]
where the time goes in v3:
time: 134 us
  Pallas kernels  122 us (91%)
  local copies, waits for them, and re-layouts  8.47 us (6%)
  other arithmetic  2.6 us (2%)
    pallas_call x1, Pallas kernels, fused(): pl.pallas_call(functools.partial(kernel, quad, cap), out_shape=(jax.Shape...  122 us
    unnamed x10, local copies, waits for them, and re-layouts  7.77 us

profile of v3, /device:TPU:0, one launch (start us, length us, event | category | flops | bytes accessed | tf_op | source)
XLA Modules:
  0.0 133.9 jit_solution(15461150429584939522)
XLA Ops:
  0.6 0.7 fusion.2
  1.3 0.1 fusion.1
  1.5 0.7 select_reduce_fusion.1
  2.2 0.6 pad_maximum_fusion.table
  2.8 0.0 copy-start.2
  2.8 122.0 %shard_map.110 = (bf16[128,2048]{1,0:T(8,128)(2,1)}, f32[2,8,128]{2,1,0:T(8,128)}, bf16[1024,768]{1,0:T(8,128)(2,1)}, bf16[1024,768]{1,0:T(8,128)(2,1)}, bf16[384,2048]{1,0:T(8,128)(2,1)}) custom-call(bf16[128,2048]{1,0:T(8,128)(2,1)} %hidden.1, bf16[128,2048]{1,0:T(8,128)(2,1)} %grad.1, f32[2,8,128]{2,1,0:T(8,128)} %pad_maximum_fusion.table, ...), custom_call_target="tpu_custom_call" | custom-call | flops 12884901888 | bytes 25165824 | tf_op jit(solution)/shard_map/pallas_call | solution.py:390
  124.8 0.7 slice.3
  125.5 0.0 copy-done.2
  125.5 0.6 select_reduce_fusion
  126.1 1.9 %copy.19 = bf16[128,2048]{1,0:T(8,128)(2,1)} copy(bf16[128,2048]{1,0:T(8,128)(2,1)} %get-tuple-element.20) | data formatting | bytes 1048576
  128.0 0.0 copy-start.1
  128.0 2.8 %copy.20 = bf16[1,1024,768]{2,1,0:T(8,128)(2,1)} copy(bf16[1,1024,768]{2,1,0:T(8,128)(2,1)} %bitcast.18) | data formatting | bytes 3145728
  130.7 0.0 copy-done.1
  130.7 0.0 copy-start
  130.7 1.1 copy.21
  131.9 0.8 copy-done
  132.7 1.1 copy.22
Async XLA Ops:
  2.8 122.7 %copy-start.2 = (s32[128,2]{0,1:T(2,128)S(1)}, s32[128,2]{0,1:T(2,128)}, u32[]{:S(2)}) copy-start(s32[128,2]{0,1:T(2,128)} %param.9) | copy-start | bytes 3076
  128.0 2.8 %copy-start.1 = (bf16[1024,768]{1,0:T(8,128)(2,1)S(1)}, bf16[1024,768]{1,0:T(8,128)(2,1)}, u32[]{:S(2)}) copy-start(bf16[1024,768]{1,0:T(8,128)(2,1)} %get-tuple-element.13) | copy-start | bytes 4718596
  130.7 2.0 %copy-start = (bf16[384,2048]{1,0:T(8,128)(2,1)S(1)}, bf16[384,2048]{1,0:T(8,128)(2,1)}, u32[]{:S(2)}) copy-start(bf16[384,2048]{1,0:T(8,128)(2,1)} %get-tuple-element.14) | copy-start | bytes 4718596

commit v4 on v3

--- a/solution.py
+++ b/solution.py
@@ -182,14 +182,11 @@
         copy.start()
         return copy
 
+    pl.semaphore_wait(barrier, quad + 1)
+    crossed = [cross(0, table.at[1 - team], far_table), cross(1, hidden, far_hidden)]
     choose(0, table[team])
     dispatch(0, hidden, send_in)
-    pl.semaphore_wait(barrier, quad + 1)
-    crossed = [cross(0, table.at[1 - team], far_table), cross(1, hidden, far_hidden)]
     in0 = spread(0, 0, send_in, rows_in, 0, width)
-    crossed.append(cross(2, grad, far_grad))
-    dispatch(0, grad, send_grad)
-    grad0 = spread(1, 0, send_grad, rows_grad, 0, width + LANE)
 
     exchanged = []
     for i, (ref, full) in enumerate(((wg, gate_full), (wu, up_full), (wd, down_full))):
@@ -203,8 +200,11 @@
         own.start()
         exchanged.append((copy, own))
 
+    dispatch(0, grad, send_grad)
     crossed[0].wait_recv()
     choose(1, far_table[...])
+    crossed[1].wait_send()
+    crossed.append(cross(2, grad, far_grad))
     crossed[1].wait_recv()
     dispatch(1, far_hidden, send_in)
     in1 = spread(0, 1, send_in, rows_in, 0, width)
@@ -221,9 +221,9 @@
             gate = dot(x, gate_full[:, cols], ((1,), (0,)))
             up = dot(x, up_full[:, cols], ((1,), (0,)))
             sigma = jax.nn.sigmoid(gate)
-            active[:, cols] = gate * sigma
-            upper[:, cols] = up
-            slope[:, cols] = up * sigma * (1.0 + gate * (1.0 - sigma))
+            active[rows, cols] = gate * sigma
+            upper[rows, cols] = up
+            slope[rows, cols] = up * sigma * (1.0 + gate * (1.0 - sigma))
             return carry
 
         lax.fori_loop(0, ff // 256, tile, 0)
@@ -235,11 +235,11 @@
         def tile(c, total):
             cols = pl.ds(pl.multiple_of(c * 256, 256), 256)
             plain = dot(rows_grad[rows, pl.ds(0, width)], down_full[cols, :], ((1,), (1,)))
-            act = active[:, cols]
-            hid = act * upper[:, cols]
+            act = active[rows, cols]
+            hid = act * upper[rows, cols]
             hidden_grad = plain * p
             up_grad[rows, cols] = (hidden_grad * act).astype(BF16)
-            gate_grad[rows, cols] = (hidden_grad * slope[:, cols]).astype(BF16)
+            gate_grad[rows, cols] = (hidden_grad * slope[rows, cols]).astype(BF16)
             scaled[rows, cols] = (hid * p).astype(BF16)
             return total + jnp.sum(hid * plain, axis=1, keepdims=True)
 
@@ -262,17 +262,20 @@
 
     arrive(in0)
     forward(0)
+    crossed[2].wait_send()
+    grad0 = spread(1, 0, send_grad, rows_grad, 0, width + LANE)
     crossed[2].wait_recv()
     dispatch(1, far_grad, send_grad)
     grad1 = spread(1, 1, send_grad, rows_grad, 0, width + LANE)
+    arrive(in1)
+    forward(1)
     arrive(grad0)
     backward(0)
     back0 = returns(0, 2, 0, width)
-    arrive(in1)
-    forward(1)
     arrive(grad1)
     backward(1)
-    back1 = [returns(1, 2, 0, half), returns(1, 3, half, half)]
+    strip = width // 4
+    back1 = [returns(1, 2 + i, i * strip, strip) for i in range(4)]
 
     def wide(which, sink, factor):
         def tile(c, carry):
@@ -330,11 +333,11 @@
 
     for i, group in enumerate(back1):
         arrive(group)
-        combine(1, relay_in, i * half, half)
-        cols = pl.ds(i * half, half)
+        combine(1, relay_in, i * strip, strip)
+        cols = pl.ds(i * strip, strip)
         crossed.append(cross(3 + i, relay_in.at[:, cols], far_in.at[:, cols]))
     relay_prob[...] = prob_table(1)
-    crossed.append(cross(5, relay_prob, far_prob))
+    crossed.append(cross(7, relay_prob, far_prob))
     wide(side, gw, gate_grad)
     wide(side, uw, up_grad)
     tall(side, dw)
@@ -351,15 +354,15 @@
 
     arrive(back0)
     prob_out[team] = prob_table(0)
-    for i in range(2):
+    for i in range(4):
         crossed[3 + i].wait_recv()
-        combine(0, in_out, i * half, half, far_in)
-    crossed[5].wait_recv()
+        combine(0, in_out, i * strip, strip, far_in)
+    crossed[7].wait_recv()
     prob_out[1 - team] = far_prob[...]
-    for copies, own in (in0, grad0, in1, grad1, back0, back1[0], back1[1]):
+    for copies, own in (in0, grad0, in1, grad1, back0, *back1):
         for copy in copies:
             copy.wait_send()
-    for copy in crossed:
+    for copy in [crossed[0]] + crossed[3:]:
         copy.wait_send()
     for copy, own in exchanged:
         copy.wait_send()
@@ -402,13 +405,13 @@
             buf(rows, width), buf(rows, width + LANE), buf(rows, width), buf(rows, width + LANE),
             buf(rows, width + LANE), buf(rows, width + LANE),
             buf(width, ff), buf(width, ff), buf(ff, width),
-            buf(rows // 2, ff, dtype=F32), buf(rows // 2, ff, dtype=F32), buf(rows // 2, ff, dtype=F32),
+            buf(rows, ff, dtype=F32), buf(rows, ff, dtype=F32), buf(rows, ff, dtype=F32),
             buf(rows, ff), buf(rows, ff), buf(rows, ff),
             buf(*wide), buf(*wide), buf(*down), buf(*wide), buf(*wide), buf(*down),
             buf(ep, tok, dtype=F32), buf(tok, width), buf(tok, width), buf(rows, tok),
             buf(tok, width), buf(tok, width), buf(ep, tok, dtype=F32), buf(ep, tok, dtype=F32),
-            dma((4, 2, quad)), dma((4, 2, quad)), dma((4, 2)),
-            dma((3,)), dma((3,)), dma((3,)), dma((3,)), dma((3,)), dma((6,)), dma((6,)),
+            dma((6, 2, quad)), dma((6, 2, quad)), dma((6, 2)),
+            dma((3,)), dma((3,)), dma((3,)), dma((3,)), dma((3,)), dma((8,)), dma((8,)),
         ],
         compiler_params=pltpu.CompilerParams(
             collective_id=0, has_side_effects=True, vmem_limit_bytes=60 << 20
@@ -426,7 +429,7 @@
     tok, top = arrays[2].shape
     width, ff = arrays[4].shape[1] * 2, arrays[4].shape[2]
     ep = lax.axis_size("ep")
-    whole_tiles = tok % 128 == 0 and width % 512 == 0 and ff % 256 == 0
+    whole_tiles = tok % 128 == 0 and width % 2048 == 0 and ff % 256 == 0
     one_each = arrays[4].shape[0] == 1 and lax.axis_size("edp") == 2
     if one_each and whole_tiles and ep == 8 and tok == LANE and 2 * tok * top // ep % 32 == 0:
         return fused(*arrays)

time: 134 us -> 137 us (1.022)
  Pallas kernels: 122 us -> 125 us
    pallas_call x1, Pallas kernels: 122 us -> 125 us  [fused(): pl.pallas_call(functools.partial(kernel, quad, cap), out_shape=(jax.Shape...]
where the time goes in v4:
time: 137 us
  Pallas kernels  125 us (91%)
  local copies, waits for them, and re-layouts  8.47 us (6%)
  other arithmetic  2.6 us (2%)
    pallas_call x1, Pallas kernels, fused(): pl.pallas_call(functools.partial(kernel, quad, cap), out_shape=(jax.Shape...  125 us
    unnamed x10, local copies, waits for them, and re-layouts  7.77 us

profile of v4, /device:TPU:0, one launch (start us, length us, event | category | flops | bytes accessed | tf_op | source)
XLA Modules:
  0.0 136.5 jit_solution(451824147475365602)
XLA Ops:
  0.6 0.7 fusion.2
  1.3 0.1 fusion.1
  1.5 0.7 select_reduce_fusion.1
  2.2 0.6 pad_maximum_fusion.table
  2.8 0.0 copy-start.2
  2.8 124.7 %shard_map.110 = (bf16[128,2048]{1,0:T(8,128)(2,1)}, f32[2,8,128]{2,1,0:T(8,128)}, bf16[1024,768]{1,0:T(8,128)(2,1)}, bf16[1024,768]{1,0:T(8,128)(2,1)}, bf16[384,2048]{1,0:T(8,128)(2,1)}) custom-call(bf16[128,2048]{1,0:T(8,128)(2,1)} %hidden.1, bf16[128,2048]{1,0:T(8,128)(2,1)} %grad.1, f32[2,8,128]{2,1,0:T(8,128)} %pad_maximum_fusion.table, ...), custom_call_target="tpu_custom_call" | custom-call | flops 12884901888 | bytes 25165824 | tf_op jit(solution)/shard_map/pallas_call | solution.py:393
  127.5 0.7 slice.3
  128.2 0.0 copy-done.2
  128.2 0.6 select_reduce_fusion
  128.7 1.9 %copy.19 = bf16[128,2048]{1,0:T(8,128)(2,1)} copy(bf16[128,2048]{1,0:T(8,128)(2,1)} %get-tuple-element.20) | data formatting | bytes 1048576
  130.6 0.0 copy-start.1
  130.6 2.8 %copy.20 = bf16[1,1024,768]{2,1,0:T(8,128)(2,1)} copy(bf16[1,1024,768]{2,1,0:T(8,128)(2,1)} %bitcast.18) | data formatting | bytes 3145728
  133.4 0.0 copy-done.1
  133.4 0.0 copy-start
  133.4 1.1 copy.21
  134.5 0.8 copy-done
  135.4 1.1 copy.22
Async XLA Ops:
  2.8 125.4 %copy-start.2 = (s32[128,2]{0,1:T(2,128)S(1)}, s32[128,2]{0,1:T(2,128)}, u32[]{:S(2)}) copy-start(s32[128,2]{0,1:T(2,128)} %param.9) | copy-start | bytes 3076
  130.6 2.8 %copy-start.1 = (bf16[1024,768]{1,0:T(8,128)(2,1)S(1)}, bf16[1024,768]{1,0:T(8,128)(2,1)}, u32[]{:S(2)}) copy-start(bf16[1024,768]{1,0:T(8,128)(2,1)} %get-tuple-element.13) | copy-start | bytes 4718596
  133.4 2.0 %copy-start = (bf16[384,2048]{1,0:T(8,128)(2,1)S(1)}, bf16[384,2048]{1,0:T(8,128)(2,1)}, u32[]{:S(2)}) copy-start(bf16[384,2048]{1,0:T(8,128)(2,1)} %get-tuple-element.14) | copy-start | bytes 4718596

commit v5 on v4

--- a/solution.py
+++ b/solution.py
@@ -187,6 +187,9 @@
     choose(0, table[team])
     dispatch(0, hidden, send_in)
     in0 = spread(0, 0, send_in, rows_in, 0, width)
+    crossed.append(cross(2, grad, far_grad))
+    dispatch(0, grad, send_grad)
+    grad0 = spread(1, 0, send_grad, rows_grad, 0, width + LANE)
 
     exchanged = []
     for i, (ref, full) in enumerate(((wg, gate_full), (wu, up_full), (wd, down_full))):
@@ -200,11 +203,8 @@
         own.start()
         exchanged.append((copy, own))
 
-    dispatch(0, grad, send_grad)
     crossed[0].wait_recv()
     choose(1, far_table[...])
-    crossed[1].wait_send()
-    crossed.append(cross(2, grad, far_grad))
     crossed[1].wait_recv()
     dispatch(1, far_hidden, send_in)
     in1 = spread(0, 1, send_in, rows_in, 0, width)
@@ -262,16 +262,14 @@
 
     arrive(in0)
     forward(0)
-    crossed[2].wait_send()
-    grad0 = spread(1, 0, send_grad, rows_grad, 0, width + LANE)
     crossed[2].wait_recv()
     dispatch(1, far_grad, send_grad)
     grad1 = spread(1, 1, send_grad, rows_grad, 0, width + LANE)
-    arrive(in1)
-    forward(1)
     arrive(grad0)
     backward(0)
     back0 = returns(0, 2, 0, width)
+    arrive(in1)
+    forward(1)
     arrive(grad1)
     backward(1)
     strip = width // 4
@@ -362,7 +360,7 @@
     for copies, own in (in0, grad0, in1, grad1, back0, *back1):
         for copy in copies:
             copy.wait_send()
-    for copy in [crossed[0]] + crossed[3:]:
+    for copy in crossed:
         copy.wait_send()
     for copy, own in exchanged:
         copy.wait_send()

time: 137 us -> 134 us (0.978)
  Pallas kernels: 125 us -> 122 us
    pallas_call x1, Pallas kernels: 125 us -> 122 us  [fused(): pl.pallas_call(functools.partial(kernel, quad, cap), out_shape=(jax.Shape...]
where the time goes in v5:
time: 134 us; the launch traced here: 133 us
  Pallas kernels  122 us (91%)
  local copies, waits for them, and re-layouts  8.47 us (6%)
  other arithmetic  2.6 us (2%)
    pallas_call x1, Pallas kernels, fused(): pl.pallas_call(functools.partial(kernel, quad, cap), out_shape=(jax.Shape...  122 us
    unnamed x10, local copies, waits for them, and re-layouts  7.77 us

profile of v5, /device:TPU:0, one launch (start us, length us, event | category | flops | bytes accessed | tf_op | source)
XLA Modules:
  0.0 133.4 jit_solution(16728443285348668006)
XLA Ops:
  0.6 0.7 fusion.2
  1.3 0.1 fusion.1
  1.5 0.7 select_reduce_fusion.1
  2.2 0.6 pad_maximum_fusion.table
  2.8 0.0 copy-start.2
  2.8 121.6 %shard_map.110 = (bf16[128,2048]{1,0:T(8,128)(2,1)}, f32[2,8,128]{2,1,0:T(8,128)}, bf16[1024,768]{1,0:T(8,128)(2,1)}, bf16[1024,768]{1,0:T(8,128)(2,1)}, bf16[384,2048]{1,0:T(8,128)(2,1)}) custom-call(bf16[128,2048]{1,0:T(8,128)(2,1)} %hidden.1, bf16[128,2048]{1,0:T(8,128)(2,1)} %grad.1, f32[2,8,128]{2,1,0:T(8,128)} %pad_maximum_fusion.table, ...), custom_call_target="tpu_custom_call" | custom-call | flops 12884901888 | bytes 25165824 | tf_op jit(solution)/shard_map/pallas_call | solution.py:391
  124.4 0.7 slice.3
  125.1 0.0 copy-done.2
  125.1 0.6 select_reduce_fusion
  125.6 1.9 %copy.19 = bf16[128,2048]{1,0:T(8,128)(2,1)} copy(bf16[128,2048]{1,0:T(8,128)(2,1)} %get-tuple-element.20) | data formatting | bytes 1048576
  127.5 0.0 copy-start.1
  127.5 2.8 %copy.20 = bf16[1,1024,768]{2,1,0:T(8,128)(2,1)} copy(bf16[1,1024,768]{2,1,0:T(8,128)(2,1)} %bitcast.18) | data formatting | bytes 3145728
  130.3 0.0 copy-done.1
  130.3 0.0 copy-start
  130.3 1.1 copy.21
  131.4 0.8 copy-done
  132.3 1.1 copy.22
Async XLA Ops:
  2.8 122.3 %copy-start.2 = (s32[128,2]{0,1:T(2,128)S(1)}, s32[128,2]{0,1:T(2,128)}, u32[]{:S(2)}) copy-start(s32[128,2]{0,1:T(2,128)} %param.9) | copy-start | bytes 3076
  127.5 2.8 %copy-start.1 = (bf16[1024,768]{1,0:T(8,128)(2,1)S(1)}, bf16[1024,768]{1,0:T(8,128)(2,1)}, u32[]{:S(2)}) copy-start(bf16[1024,768]{1,0:T(8,128)(2,1)} %get-tuple-element.13) | copy-start | bytes 4718596
  130.3 2.0 %copy-start = (bf16[384,2048]{1,0:T(8,128)(2,1)S(1)}, bf16[384,2048]{1,0:T(8,128)(2,1)}, u32[]{:S(2)}) copy-start(bf16[384,2048]{1,0:T(8,128)(2,1)} %get-tuple-element.14) | copy-start | bytes 4718596

commit v6 on v5

--- a/solution.py
+++ b/solution.py
@@ -301,13 +301,7 @@
         copy.start()
         return copy
 
-    wide(other, gate_send, gate_grad)
-    passed = [pass_on(0, gate_send, gate_got)]
-    wide(other, up_send, up_grad)
-    passed.append(pass_on(1, up_send, up_got))
-    tall(other, down_send)
-    passed.append(pass_on(2, down_send, down_got))
-
+    passed = []
     def combine(part, sink, low, size, extra=None):
         rows = pl.ds(part * part_rows, part_rows)
 
@@ -334,6 +328,15 @@
         combine(1, relay_in, i * strip, strip)
         cols = pl.ds(i * strip, strip)
         crossed.append(cross(3 + i, relay_in.at[:, cols], far_in.at[:, cols]))
+        if i == 0:
+            wide(other, gate_send, gate_grad)
+            passed.append(pass_on(0, gate_send, gate_got))
+        elif i == 1:
+            wide(other, up_send, up_grad)
+            passed.append(pass_on(1, up_send, up_got))
+        elif i == 2:
+            tall(other, down_send)
+            passed.append(pass_on(2, down_send, down_got))
     relay_prob[...] = prob_table(1)
     crossed.append(cross(7, relay_prob, far_prob))
     wide(side, gw, gate_grad)

time: 134 us -> 134 us (level)
  no operation moved by 1% of the time
where the time goes in v6:
time: 134 us; the launch traced here: 133 us
  Pallas kernels  122 us (91%)
  local copies, waits for them, and re-layouts  8.47 us (6%)
  other arithmetic  2.6 us (2%)
    pallas_call x1, Pallas kernels, fused(): pl.pallas_call(functools.partial(kernel, quad, cap), out_shape=(jax.Shape...  122 us
    unnamed x10, local copies, waits for them, and re-layouts  7.77 us

profile of v6, /device:TPU:0, one launch (start us, length us, event | category | flops | bytes accessed | tf_op | source)
XLA Modules:
  0.0 133.4 jit_solution(7949042568047896833)
XLA Ops:
  0.6 0.7 fusion.2
  1.3 0.1 fusion.1
  1.5 0.7 select_reduce_fusion.1
  2.2 0.6 pad_maximum_fusion.table
  2.8 0.0 copy-start.2
  2.8 121.6 %shard_map.110 = (bf16[128,2048]{1,0:T(8,128)(2,1)}, f32[2,8,128]{2,1,0:T(8,128)}, bf16[1024,768]{1,0:T(8,128)(2,1)}, bf16[1024,768]{1,0:T(8,128)(2,1)}, bf16[384,2048]{1,0:T(8,128)(2,1)}) custom-call(bf16[128,2048]{1,0:T(8,128)(2,1)} %hidden.1, bf16[128,2048]{1,0:T(8,128)(2,1)} %grad.1, f32[2,8,128]{2,1,0:T(8,128)} %pad_maximum_fusion.table, ...), custom_call_target="tpu_custom_call" | custom-call | flops 12884901888 | bytes 25165824 | tf_op jit(solution)/shard_map/pallas_call | solution.py:394
  124.4 0.7 slice.3
  125.1 0.0 copy-done.2
  125.1 0.6 select_reduce_fusion
  125.6 1.9 %copy.19 = bf16[128,2048]{1,0:T(8,128)(2,1)} copy(bf16[128,2048]{1,0:T(8,128)(2,1)} %get-tuple-element.20) | data formatting | bytes 1048576
  127.5 0.0 copy-start.1
  127.5 2.8 %copy.20 = bf16[1,1024,768]{2,1,0:T(8,128)(2,1)} copy(bf16[1,1024,768]{2,1,0:T(8,128)(2,1)} %bitcast.18) | data formatting | bytes 3145728
  130.3 0.0 copy-done.1
  130.3 0.0 copy-start
  130.3 1.1 copy.21
  131.4 0.8 copy-done
  132.3 1.1 copy.22
Async XLA Ops:
  2.8 122.3 %copy-start.2 = (s32[128,2]{0,1:T(2,128)S(1)}, s32[128,2]{0,1:T(2,128)}, u32[]{:S(2)}) copy-start(s32[128,2]{0,1:T(2,128)} %param.9) | copy-start | bytes 3076
  127.5 2.8 %copy-start.1 = (bf16[1024,768]{1,0:T(8,128)(2,1)S(1)}, bf16[1024,768]{1,0:T(8,128)(2,1)}, u32[]{:S(2)}) copy-start(bf16[1024,768]{1,0:T(8,128)(2,1)} %get-tuple-element.13) | copy-start | bytes 4718596
  130.3 2.0 %copy-start = (bf16[384,2048]{1,0:T(8,128)(2,1)S(1)}, bf16[384,2048]{1,0:T(8,128)(2,1)}, u32[]{:S(2)}) copy-start(bf16[384,2048]{1,0:T(8,128)(2,1)} %get-tuple-element.14) | copy-start | bytes 4718596
